TPU v7x, 256 devices: a whole 4x4x8 slice. The times are simulated.
256 devices in a mesh: lon: 8 (over z), lat: 16 (over y, x), span: 2 (over core).
Axes of the slice: x: 4, y: 4, z: 8, core: 2. Of those that a mesh axis runs over, the one named last changes fastest.
Arguments:
- state: float32 [2, 64, 256, 4096], P(None, None, 'lat', ('lon', 'span')), may hold values from -6 to 6
- winds: float32 [2, 64, 256, 4096], P(None, None, 'lat', ('lon', 'span')), may hold values from -0.45 to 0.45
- memory: bfloat16 [1048576, 128], P(('lon', 'lat', 'span')), may hold values from -6 to 6
- w_in: bfloat16 [256, 512], replicated, may hold values from -0.375 to 0.375
- w_mid: bfloat16 [512, 512], replicated, may hold values from -0.25 to 0.25
- w_deep: bfloat16 [512, 512], replicated, may hold values from -0.25 to 0.25
- w_out: bfloat16 [512, 256], replicated, may hold values from -0.25 to 0.25
- dest: int32 [256, 4096], P('lat', ('lon', 'span')), may hold values from 0 to 31, as said below
- slot: int32 [256, 4096], P('lat', ('lon', 'span')), may hold values from 0 to 127, as said below
- convect: int32 [256, 4096], P('lat', ('lon', 'span')), may hold values from 0 to 1
Outputs:
- new_state: float32 [2, 64, 256, 4096], P(None, None, 'lat', ('lon', 'span'))
- new_memory: bfloat16 [1048576, 128], P(('lon', 'lat', 'span'))
Inputs may be any that keep to these rules, and one draw needn't show every extreme that they name: `dest`: owner of a column among the 32 devices of the same lon index, numbered lat index * 2 + span index. The columns of one device with convect 1 and one owner hold slots 0 to n - 1, each once, with n at most 128; in every lon index some owner gets exactly 128 such columns from every device. `slot`: slot of a column at its owner, see dest.
All inputs are finite; a program needn't handle non-finite values.
Results may differ from a plain program's by a relative error of at most 0.003.
Values may be sent and summed in bfloat16 or wider, within the bound.
No kernel may reach another device: no remote copies, remote signals or barrier semaphores. Data moves between devices by JAX's collectives and lax.ppermute only.
A program may use at most 64 MiB of HBM per device.

v0:
```python
import jax
import jax.numpy as jnp
from jax import lax
from jax.sharding import PartitionSpec as P


def padded(shard, sides, width, wrap):
    for axis, dim in sides:
        count, length = (lax.axis_size(axis), shard.shape[dim])
        up = [(i, (i + 1) % count) for i in range(count if wrap else count - 1)]
        down = [(j, i) for i, j in up]
        last = lax.slice_in_dim(shard, length - width, length, axis=dim)
        first = lax.slice_in_dim(shard, 0, width, axis=dim)
        before = lax.ppermute(last, axis, up)
        after = lax.ppermute(first, axis, down)
        shard = jnp.concatenate([before, shard, after], axis=dim)
    return shard


def advect(state, winds):
    beside_lat = padded(state.astype(jnp.bfloat16), (("lat", 2),), 1, False).astype(state.dtype)
    beside_lon = padded(state.astype(jnp.bfloat16), ((("lon", "span"), 3),), 1, True).astype(
        state.dtype
    )
    west = beside_lon[:, :, :, :-2]
    east = beside_lon[:, :, :, 2:]
    south = beside_lat[:, :, :-2, :]
    north = beside_lat[:, :, 2:, :]
    zonal = winds[0][None]
    meridional = winds[1][None]
    return (
        state
        - jnp.maximum(zonal, 0.0) * (state - west)
        - jnp.minimum(zonal, 0.0) * (east - state)
        - jnp.maximum(meridional, 0.0) * (state - south)
        - jnp.minimum(meridional, 0.0) * (north - state)
    )


def column_mlp(columns, recalled, w_in, w_mid, w_deep, w_out):
    joined = jnp.concatenate([columns, recalled], axis=1)
    first = jax.nn.silu(jnp.dot(joined, w_in, preferred_element_type=jnp.float32)).astype(
        jnp.bfloat16
    )
    second = jax.nn.silu(jnp.dot(first, w_mid, preferred_element_type=jnp.float32)).astype(
        jnp.bfloat16
    )
    third = jax.nn.silu(jnp.dot(second, w_deep, preferred_element_type=jnp.float32)).astype(
        jnp.bfloat16
    )
    result = jnp.dot(third, w_out, preferred_element_type=jnp.float32)
    width = columns.shape[1]
    tendency = result[:, :width].astype(jnp.bfloat16)
    renewed = (recalled.astype(jnp.float32) + result[:, width:]).astype(jnp.bfloat16)
    return (tendency, renewed)


def move_pair(rows, flags):
    got_rows, got_flags = (
        lax.all_to_all(rows, ("lat", "span"), split_axis=0, concat_axis=0, tiled=True),
        lax.all_to_all(flags, ("lat", "span"), split_axis=0, concat_axis=0, tiled=True),
    )
    return (got_rows, got_flags)


def move_one(rows):
    return lax.all_to_all(rows, ("lat", "span"), split_axis=0, concat_axis=0, tiled=True)


def place_rows(values, source_of, filled):
    picked = values[jnp.minimum(source_of, values.shape[0] - 1)]
    return jnp.where(filled[:, None], picked, jnp.zeros_like(picked))


def body(state, winds, memory, w_in, w_mid, w_deep, w_out, dest, slot, convect):
    fields, levels, rows_lat, rows_lon = state.shape
    count = rows_lat * rows_lon
    width = fields * levels
    group = lax.axis_size("lat") * lax.axis_size("span")
    capacity = count // group
    columns = state.reshape(width, count).T.astype(jnp.bfloat16)
    live = convect.reshape(count) > 0
    target = dest.reshape(count) * capacity + slot.reshape(count)
    parked = jnp.where(live, target, count)
    positions = jnp.arange(count, dtype=jnp.int32)
    source_of = jnp.full((count,), count, jnp.int32).at[parked].set(positions, mode="drop")
    filled = source_of < count
    flags = filled.astype(jnp.bfloat16)
    dynamics = advect(state, winds)
    outgoing = place_rows(columns, source_of, filled)
    arrived, arrived_flags = move_pair(outgoing, flags)
    owner_tend, renewed = column_mlp(arrived, memory, w_in, w_mid, w_deep, w_out)
    new_memory = jnp.where(arrived_flags[:, None] > 0, renewed, memory)
    local_tend = move_one(owner_tend)[target]
    change = jnp.where(live[:, None], local_tend.astype(jnp.float32), 0.0)
    new_state = dynamics + change.T.reshape(fields, levels, rows_lat, rows_lon)
    return (new_state, new_memory)


def solution(mesh):
    in_specs = (
        P(None, None, "lat", ("lon", "span")),
        P(None, None, "lat", ("lon", "span")),
        P(("lon", "lat", "span"), None),
        P(),
        P(),
        P(),
        P(),
        P("lat", ("lon", "span")),
        P("lat", ("lon", "span")),
        P("lat", ("lon", "span")),
    )
    out_specs = (P(None, None, "lat", ("lon", "span")), P(("lon", "lat", "span"), None))
    return jax.shard_map(body, mesh=mesh, in_specs=in_specs, out_specs=out_specs, check_vma=False)
```

profile of v0, /device:TPU:2, one launch (start us, length us, event | category | flops | bytes accessed | tf_op | source)
XLA Modules:
  0.0 141.5 jit_solution(785071326154792456)
XLA Ops:
  2.9 15.5 %scatter_custom_fusion = s32[4096]{0:T(1024)S(1)} fusion(s32[4096]{0:T(1024)S(1)} %bitcast.57, s32[4096]{0:T(1024)S(1)} %iota.3, s32[]{:T(128)} %constant.9.clone.1), kind=kCustom, calls=%fused_computation.47 | custom fusion | bytes 16388 | tf_op jit(solution)/shard_map/scatter | solution.py:86
  19.0 7.6 %all-to-all-start.2 = ((bf16[32,128,1]{1,2,0:T(2,128)(2,1)}), bf16[32,128,1]{1,2,0:T(2,128)(2,1)S(1)}, u32[]{:S(2)}, u32[]{:S(2)}) async-start(bf16[32,128,1]{1,2,0:T(2,128)(2,1)} %copy.18), calls=%async_computation.2 | async-start | bytes 32768 | tf_op jit(solution)/shard_map/all_to_all | solution.py:61
  26.7 1.7 %convert_element_type.39 = bf16[2,64,16,256]{3,2,1,0:T(8,128)(2,1)S(1)} convert(f32[2,64,16,256]{3,2,1,0:T(8,128)} %param.10) | non-fusion elementwise | flops 524288 | bytes 3145728 | tf_op jit(solution)/shard_map/convert_element_type | solution.py:22
  29.8 1.6 %copy.16 = bf16[128,4096]{0,1:T(8,128)(2,1)S(1)} copy(bf16[128,4096]{1,0:T(8,128)(2,1)} %bitcast.50) | data formatting | bytes 2097152 | tf_op jit(solution)/shard_map/convert_element_type | solution.py:81
  31.4 15.0 %gather_fusion = bf16[4096,128]{1,0:T(8,128)(2,1)} fusion(bf16[4096,128]{1,0:T(8,128)(2,1)S(1)} %bitcast.45, s32[4096]{0:T(1024)S(1)} %fusion.21), kind=kCustom, calls=%fused_computation | custom fusion | bytes 2113536 | tf_op jit(solution)/shard_map/gather | solution.py:71
  46.4 2.5 %broadcast_select_fusion = bf16[32,128,128]{2,1,0:T(8,128)(2,1)} fusion(bf16[32,128,128]{2,1,0:T(8,128)(2,1)} %bitcast.49, pred[32,128]{1,0:T(8,128)(4,1)S(1)} %bitcast.56), kind=kLoop, calls=%fused_computation.37 | loop fusion | flops 524288 | bytes 2101248 | tf_op jit(solution)/shard_map/jit(_where)/select_n | solution.py:72
  49.0 7.4 %all-to-all-start = ((bf16[32,128,128]{2,1,0:T(8,128)(2,1)}), bf16[32,128,128]{2,1,0:T(8,128)(2,1)S(1)}, u32[]{:S(2)}, u32[]{:S(2)}) async-start(bf16[32,128,128]{2,1,0:T(8,128)(2,1)} %broadcast_select_fusion), calls=%async_computation | async-start | bytes 2097152 | tf_op jit(solution)/shard_map/all_to_all | solution.py:60
  57.7 5.5 %collective-permute-start.1 = (bf16[2,64,16,1]{3,2,1,0:T(8,128)(2,1)}, bf16[2,64,16,1]{3,2,1,0:T(8,128)(2,1)}, u32[]{:S(2)}, u32[]{:S(2)}) collective-permute-start(bf16[2,64,16,1]{3,2,1,0:T(8,128)(2,1)} %get-tuple-element.11), channel_id=1, source_target_pairs={{1,0},{32,1},{33,32},{64,33},{65,64},{96,65},{97,96},{128,97},{129... | collective-permute-start | bytes 12296 | tf_op jit(solution)/shard_map/ppermute | solution.py:15
  64.1 3.4 %collective-permute-start.2 = (bf16[2,64,1,256]{3,2,1,0:T(2,128)(2,1)}, bf16[2,64,1,256]{3,2,1,0:T(2,128)(2,1)S(1)}, u32[]{:S(2)}, u32[]{:S(2)}) collective-permute-start(bf16[2,64,1,256]{3,2,1,0:T(2,128)(2,1)} %get-tuple-element.12), channel_id=1, source_target_pairs={{0,2},{2,4},{4,6},{6,8},{8,10},{10,12},{12,14},{14,16},{16,18},{18... | collective-permute-start | bytes 196616 | tf_op jit(solution)/shard_map/ppermute | solution.py:14
  67.4 2.5 %collective-permute-start.3 = (bf16[2,64,1,256]{3,2,1,0:T(2,128)(2,1)S(1)}, bf16[2,64,1,256]{3,2,1,0:T(2,128)(2,1)S(1)}, u32[]{:S(2)}, u32[]{:S(2)}) collective-permute-start(bf16[2,64,1,256]{3,2,1,0:T(2,128)(2,1)S(1)} %get-tuple-element.13), channel_id=1, source_target_pairs={{2,0},{4,2},{6,4},{8,6},{10,8},{12,10},{14,12},{16,14},{18,16},{20... | collective-permute-start | bytes 196616 | tf_op jit(solution)/shard_map/ppermute | solution.py:15
  70.5 2.1 %all-to-all-done = bf16[32,128,128]{2,1,0:T(8,128)(2,1)S(1)} async-done(((bf16[32,128,128]{2,1,0:T(8,128)(2,1)}), bf16[32,128,128]{2,1,0:T(8,128)(2,1)S(1)}, u32[]{:S(2)}, u32[]{:S(2)}) %all-to-all-start) | async-done | bytes 1048608 | tf_op jit(solution)/shard_map/all_to_all | solution.py:60
  72.6 7.5 %fusion = f32[4096,512]{1,0:T(8,128)} fusion(bf16[512,512]{1,0:T(8,128)(2,1)S(1)} %copy-done, bf16[256,512]{1,0:T(8,128)(2,1)} %param.13, bf16[4096,128]{1,0:T(8,128)(2,1)} %param.12, bf16[4096,128]{1,0:T(8,128)(2,1)S(1)} %bitcast.52), kind=kOutput, calls=%fused_computation.6 | convolution fusion | flops 3235905536 | bytes 11272192 | tf_op jit(solution)/shard_map/dot_general | solution.py:45
  80.1 9.6 %fusion.2 = f32[4096,256]{1,0:T(8,128)} fusion(bf16[512,256]{1,0:T(8,128)(2,1)} %param.16, bf16[512,512]{1,0:T(8,128)(2,1)} %param.15, f32[4096,512]{1,0:T(8,128)} %fusion), kind=kOutput, calls=%fused_computation.8 | convolution fusion | flops 3242196992 | bytes 13369344 | tf_op jit(solution)/shard_map/dot_general | solution.py:51
  89.7 3.5 %fusion.20 = (bf16[4096,128]{1,0:T(8,128)(2,1)}, bf16[4096,128]{1,0:T(8,128)(2,1)}) fusion(bf16[4096,128]{1,0:T(8,128)(2,1)S(1)} %copy-done.4, f32[4096,256]{1,0:T(8,128)} %fusion.2, pred[4096]{0:T(1024)(128)(4,1)S(1)} %copy-done.7), kind=kLoop, calls=%fused_computation.30 | loop fusion | flops 2097152 | bytes 6295552 | tf_op jit(solution)/shard_map/jit(_where)/select_n | solution.py:93
  93.2 5.3 %all-to-all-start.1 = ((bf16[32,128,128]{2,1,0:T(8,128)(2,1)}), bf16[32,128,128]{2,1,0:T(8,128)(2,1)S(1)}, u32[]{:S(2)}, u32[]{:S(2)}) async-start(bf16[32,128,128]{2,1,0:T(8,128)(2,1)} %bitcast.51), calls=%async_computation.1 | async-start | bytes 2097152 | tf_op jit(solution)/shard_map/all_to_all | solution.py:67
  99.3 3.8 %maximum_bitcast_fusion.1 = (f32[64,16,256]{2,1,0:T(8,128)}, f32[64,16,256]{2,1,0:T(8,128)}, f32[64,16,256]{2,1,0:T(8,128)}, f32[64,16,256]{2,1,0:T(8,128)}) fusion(f32[2,64,16,256]{3,2,1,0:T(8,128)} %param.11), kind=kLoop, calls=%fused_computation.36 | loop fusion | flops 1048576 | bytes 6291456 | tf_op jit(solution)/shard_map/mul | solution.py:33
  105.0 3.5 %maximum_convert_fusion = f32[2,64,16,258]{3,2,1,0:T(8,128)} fusion(bf16[2,64,16,1]{3,2,1,0:T(8,128)(2,1)} %collective-permute-done.1, bf16[2,64,16,256]{3,2,1,0:T(8,128)(2,1)S(1)} %convert_element_type.39, bf16[2,64,16,1]{3,2,1,0:T(8,128)(2,1)S(1)} %collective-permute-done), kind=kLoop, calls=%fused_computation.31 | loop fusion | flops 3170304 | bytes 3170304 | tf_op jit(solution)/shard_map/convert_element_type | solution.py:22
  108.5 2.4 %maximum_convert_fusion.1 = f32[2,64,18,256]{3,2,1,0:T(8,128)} fusion(bf16[2,64,1,256]{3,2,1,0:T(2,128)(2,1)S(1)} %collective-permute-done.3, bf16[2,64,16,256]{3,2,1,0:T(8,128)(2,1)S(1)} %convert_element_type.39, bf16[2,64,1,256]{3,2,1,0:T(2,128)(2,1)S(1)} %collective-permute-done.2), kind=kLoop, calls=%fused_computation.32 | loop fusion | flops 3538944 | bytes 3538944 | tf_op jit(solution)/shard_map/convert_element_type | solution.py:21
  111.0 3.7 %all-to-all-done.1 = bf16[32,128,128]{2,1,0:T(8,128)(2,1)S(1)} async-done(((bf16[32,128,128]{2,1,0:T(8,128)(2,1)}), bf16[32,128,128]{2,1,0:T(8,128)(2,1)S(1)}, u32[]{:S(2)}, u32[]{:S(2)}) %all-to-all-start.1) | async-done | bytes 1048608 | tf_op jit(solution)/shard_map/all_to_all | solution.py:67
  114.7 12.1 %gather_fusion.1 = bf16[4096,128]{1,0:T(8,128)(2,1)S(1)} fusion(bf16[4096,128]{1,0:T(8,128)(2,1)S(1)} %bitcast.44, s32[4096]{0:T(1024)S(1)} %broadcast_clamp_fusion), kind=kCustom, calls=%fused_computation.1 | custom fusion | bytes 2113536 | tf_op jit(solution)/shard_map/gather | solution.py:94
  126.8 3.1 %select_bitcast_fusion = f32[128,4096]{0,1:T(8,128)} fusion(bf16[4096,128]{1,0:T(8,128)(2,1)S(1)} %gather_fusion.1, pred[4096]{0:T(1024)(128)(4,1)S(1)} %copy-done.6), kind=kLoop, calls=%fused_computation.29 | loop fusion | flops 1048576 | bytes 3149824 | tf_op jit(solution)/shard_map/jit(_where)/select_n | solution.py:95
  129.9 3.0 %copy.17 = f32[128,4096]{1,0:T(8,128)} copy(f32[128,4096]{0,1:T(8,128)} %select_bitcast_fusion) | data formatting | bytes 4194304 | tf_op jit(solution)/shard_map/jit(_where)/select_n | solution.py:95
  133.0 2.4 %copy.23 = f32[16,8,16,256]{3,2,1,0:T(8,128)S(1)} copy(f32[16,8,16,256]{3,1,2,0:T(8,128)} %bitcast.48) | data formatting | bytes 4194304
  135.8 5.7 %bitcast_add_fusion = f32[2,64,16,256]{3,2,1,0:T(8,128)} fusion(f32[2,64,16,256]{3,2,1,0:T(8,128)} %param.10, f32[2,64,18,256]{3,2,1,0:T(8,128)} %maximum_convert_fusion.1, f32[2,64,16,258]{3,2,1,0:T(8,128)S(1)} %copy-done.1, f32[64,16,256]{2,1,0:T(8,128)} %get-tuple-element.8, f32[64,16,256]{2,1,0:T(8,128)} %get-tuple-element.9, ...), kind=kLoop, calls=%fused_computation.10 | loop fusion | flops 6815744 | bytes 18874368 | tf_op jit(solution)/shard_map/add | solution.py:96
  (38 shorter events, 10.1 us)
Async XLA Ops:
  0.6 72.0 %copy-start = (bf16[512,512]{1,0:T(8,128)(2,1)S(1)}, bf16[512,512]{1,0:T(8,128)(2,1)}, u32[]{:S(2)}) copy-start(bf16[512,512]{1,0:T(8,128)(2,1)} %param.14) | copy-start | bytes 1572868
  19.0 29.9 %all-to-all-start.2 = ((bf16[32,128,1]{1,2,0:T(2,128)(2,1)}), bf16[32,128,1]{1,2,0:T(2,128)(2,1)S(1)}, u32[]{:S(2)}, u32[]{:S(2)}) async-start(bf16[32,128,1]{1,2,0:T(2,128)(2,1)} %copy.18), calls=%async_computation.2 | async-start | bytes 32768 | tf_op jit(solution)/shard_map/all_to_all | solution.py:61
  49.0 23.6 %all-to-all-start = ((bf16[32,128,128]{2,1,0:T(8,128)(2,1)}), bf16[32,128,128]{2,1,0:T(8,128)(2,1)S(1)}, u32[]{:S(2)}, u32[]{:S(2)}) async-start(bf16[32,128,128]{2,1,0:T(8,128)(2,1)} %broadcast_select_fusion), calls=%async_computation | async-start | bytes 2097152 | tf_op jit(solution)/shard_map/all_to_all | solution.py:60
  57.6 47.4 %collective-permute-start = (bf16[2,64,16,1]{3,2,1,0:T(8,128)(2,1)}, bf16[2,64,16,1]{3,2,1,0:T(8,128)(2,1)S(1)}, u32[]{:S(2)}, u32[]{:S(2)}) collective-permute-start(bf16[2,64,16,1]{3,2,1,0:T(8,128)(2,1)} %get-tuple-element.10), channel_id=1, source_target_pairs={{0,1},{1,32},{32,33},{33,64},{64,65},{65,96},{96,97},{97,128},{128... | collective-permute-start | bytes 12296 | tf_op jit(solution)/shard_map/ppermute | solution.py:14
  57.7 47.3 %collective-permute-start.1 = (bf16[2,64,16,1]{3,2,1,0:T(8,128)(2,1)}, bf16[2,64,16,1]{3,2,1,0:T(8,128)(2,1)}, u32[]{:S(2)}, u32[]{:S(2)}) collective-permute-start(bf16[2,64,16,1]{3,2,1,0:T(8,128)(2,1)} %get-tuple-element.11), channel_id=1, source_target_pairs={{1,0},{32,1},{33,32},{64,33},{65,64},{96,65},{97,96},{128,97},{129... | collective-permute-start | bytes 12296 | tf_op jit(solution)/shard_map/ppermute | solution.py:15
  64.1 44.5 %collective-permute-start.2 = (bf16[2,64,1,256]{3,2,1,0:T(2,128)(2,1)}, bf16[2,64,1,256]{3,2,1,0:T(2,128)(2,1)S(1)}, u32[]{:S(2)}, u32[]{:S(2)}) collective-permute-start(bf16[2,64,1,256]{3,2,1,0:T(2,128)(2,1)} %get-tuple-element.12), channel_id=1, source_target_pairs={{0,2},{2,4},{4,6},{6,8},{8,10},{10,12},{12,14},{14,16},{16,18},{18... | collective-permute-start | bytes 196616 | tf_op jit(solution)/shard_map/ppermute | solution.py:14
  67.4 41.1 %collective-permute-start.3 = (bf16[2,64,1,256]{3,2,1,0:T(2,128)(2,1)S(1)}, bf16[2,64,1,256]{3,2,1,0:T(2,128)(2,1)S(1)}, u32[]{:S(2)}, u32[]{:S(2)}) collective-permute-start(bf16[2,64,1,256]{3,2,1,0:T(2,128)(2,1)S(1)} %get-tuple-element.13), channel_id=1, source_target_pairs={{2,0},{4,2},{6,4},{8,6},{10,8},{12,10},{14,12},{16,14},{18,16},{20... | collective-permute-start | bytes 196616 | tf_op jit(solution)/shard_map/ppermute | solution.py:15
  80.1 9.6 %copy-start.4 = (bf16[4096,128]{1,0:T(8,128)(2,1)S(1)}, bf16[4096,128]{1,0:T(8,128)(2,1)}, u32[]{:S(2)}) copy-start(bf16[4096,128]{1,0:T(8,128)(2,1)} %param.12) | copy-start | bytes 3145732
  80.1 9.6 %copy-start.7 = (pred[4096]{0:T(1024)(128)(4,1)S(1)}, pred[4096]{0:T(1024)(128)(4,1)}, u32[]{:S(2)}) copy-start(pred[4096]{0:T(1024)(128)(4,1)} %compare_bitcast_fusion) | copy-start | bytes 12292
  93.2 21.4 %all-to-all-start.1 = ((bf16[32,128,128]{2,1,0:T(8,128)(2,1)}), bf16[32,128,128]{2,1,0:T(8,128)(2,1)S(1)}, u32[]{:S(2)}, u32[]{:S(2)}) async-start(bf16[32,128,128]{2,1,0:T(8,128)(2,1)} %bitcast.51), calls=%async_computation.1 | async-start | bytes 2097152 | tf_op jit(solution)/shard_map/all_to_all | solution.py:67
  99.3 3.8 %copy-start.5 = (s32[16,256]{1,0:T(8,128)S(1)}, s32[16,256]{1,0:T(8,128)}, u32[]{:S(2)}) copy-start(s32[16,256]{1,0:T(8,128)} %param.19) | copy-start | bytes 49156
  114.7 12.1 %copy-start.6 = (pred[4096]{0:T(1024)(128)(4,1)S(1)}, pred[4096]{0:T(1024)(128)(4,1)}, u32[]{:S(2)}) copy-start(pred[4096]{0:T(1024)(128)(4,1)} %gt.34) | copy-start | bytes 12292
  129.9 5.4 %copy-start.3 = (f32[64,16,256]{2,1,0:T(8,128)S(1)}, f32[64,16,256]{2,1,0:T(8,128)}, u32[]{:S(2)}) copy-start(f32[64,16,256]{2,1,0:T(8,128)} %get-tuple-element.7) | copy-start | bytes 3145732
  133.0 2.5 %copy-start.1 = (f32[2,64,16,258]{3,2,1,0:T(8,128)S(1)}, f32[2,64,16,258]{3,2,1,0:T(8,128)}, u32[]{:S(2)}) copy-start(f32[2,64,16,258]{3,2,1,0:T(8,128)} %maximum_convert_fusion) | copy-start | bytes 6340612
  133.0 2.8 %copy-start.2 = (f32[64,16,256]{2,1,0:T(8,128)S(1)}, f32[64,16,256]{2,1,0:T(8,128)}, u32[]{:S(2)}) copy-start(f32[64,16,256]{2,1,0:T(8,128)} %get-tuple-element.6) | copy-start | bytes 3145732
where the time goes:
time: 144 us; the launch traced here: 141 us
  local copies, waits for them, and re-layouts  55.5 us (39%)
  starting transfers between devices  31.8 us (22%)
  other arithmetic  30.5 us (21%)
  matrix products  17.1 us (12%)
  waiting for transfers between devices  5.76 us (4%)
    scatter x1, local copies, waits for them, and re-layouts, body(): jnp.full((count,), count, jnp.int32).at[parked].set(positions, mode='drop')  15.5 us
    gather x1, local copies, waits for them, and re-layouts, place_rows(): picked = values[jnp.minimum(source_of, values.shape[0] - 1)]  15 us
    gather x1, local copies, waits for them, and re-layouts, body(): local_tend = move_one(owner_tend)[target]  12.1 us
    dot_general x1, matrix products, column_mlp(): result = jnp.dot(third, w_out, preferred_element_type=jnp.float32)  9.61 us
    ppermute x2, starting transfers between devices, padded(): after = lax.ppermute(first, axis, down)  7.94 us
    all_to_all x1, starting transfers between devices, move_pair(): lax.all_to_all(flags, ('lat', 'span'), split_axis=0, concat_axis=0, tiled...  7.62 us
    dot_general x1, matrix products, column_mlp(): jnp.dot(first, w_mid, preferred_element_type=jnp.float32)  7.5 us
    all_to_all x1, starting transfers between devices, move_pair(): lax.all_to_all(rows, ('lat', 'span'), split_axis=0, concat_axis=0, tiled=...  7.38 us
  transfers between devices with their start and end apart: 7, of which 2 were waited for; matrix products, arithmetic and copies ran while one was open for 41% of the time, Pallas kernels for 0%

commit v1 on v0

v1 whole, which is shorter than its diff:
```python
import jax
import jax.numpy as jnp
from jax import lax
from jax.experimental import pallas as pl
from jax.experimental.pallas import tpu as pltpu
from jax.sharding import PartitionSpec as P

GROUP_AXES = ("lat", "span")
MIB = 1024 * 1024
ROWS_MLP = 2048
PART = 1024
VMEM_LIMIT = 60 * MIB
SUB = 8


def swapped(edge, axis, first, wrap):
    count = lax.axis_size(axis)
    pairs = [(i, (i + 1) % count) for i in range(first, count if wrap else count - 1, 2)]
    return lax.ppermute(edge, axis, pairs + [(j, i) for i, j in pairs])


def exchange(rows):
    return lax.all_to_all(rows, GROUP_AXES, split_axis=0, concat_axis=0, tiled=True)


def tile_row(y, half):
    return (y // SUB) * (2 * SUB) + half * SUB + y % SUB


def one_hot(index, size):
    place = lax.broadcasted_iota(jnp.int32, (size, index.shape[1]), 0)
    return (place == index).astype(jnp.bfloat16)


def log2(size):
    return size.bit_length() - 1


def dispatch_kernel(
    ny,
    nx,
    dest,
    slot,
    convect,
    state_hbm,
    slots,
    lat_even,
    lat_odd,
    lon_even,
    lon_odd,
    target,
    filled,
    state,
    chosen,
    choice,
    total,
    edges,
    arrived,
):
    load = pltpu.make_async_copy(state_hbm, state, arrived)
    load.start()
    width = state.shape[0] // (ny * 2)
    lanes = nx // 2
    lower = choice.shape[1]
    uppers = chosen.shape[2] // width
    depth = choice.shape[2]
    lines = depth // nx
    steps = ny // lines
    group = filled.shape[0]
    capacity = ny * nx // group
    shift, mask = log2(lower), lower - 1
    live = convect[...] > 0
    goal = jnp.where(live, dest[...] * capacity + slot[...], ny * nx)
    owner = goal >> log2(capacity)
    owners = lax.broadcasted_iota(jnp.int32, (group, nx), 0)
    counts = jnp.zeros((group, nx), jnp.int32)
    for y in range(ny):
        counts += (owners == owner[y : y + 1]).astype(jnp.int32)
    filled[...] = jnp.broadcast_to(jnp.sum(counts, axis=1, keepdims=True), filled.shape)
    for half in range(2):
        target[half] = goal[:, half * lanes : (half + 1) * lanes]
    goals = goal.T
    load.wait()

    def build(g, b):
        for line in range(lines):
            y = g * lines + line
            choice[b, :, pl.ds(line * nx, nx)] = one_hot(goal[y : y + 1] & mask, lower)
            upper = jnp.broadcast_to(goals[:, y : y + 1] >> shift, (nx, width))
            for half in range(2):
                part = slice(half * lanes, (half + 1) * lanes)
                values = state[pl.ds(tile_row(y, half), width, stride=2 * ny), :].T
                if half == 0:
                    edges[pl.ds(y, 1), :] = values[:1]
                else:
                    edges[pl.ds(ny + y, 1), :] = values[lanes - 1 :]
                values = values.astype(jnp.bfloat16)
                rows = pl.ds(line * nx + half * lanes, lanes)
                for h in range(uppers):
                    chosen[b, rows, pl.ds(h * width, width)] = jnp.where(
                        upper[part] == h, values, jnp.zeros_like(values)
                    )

    def multiply(g, b):
        product = jnp.dot(choice[b], chosen[b], preferred_element_type=jnp.float32)
        if g == 0:
            total[...] = product
        else:
            total[...] += product

    build(0, 0)
    for g in range(steps):
        if g < steps - 1:
            build(g + 1, (g + 1) % 2)
        multiply(g, g % 2)
    for h in range(uppers):
        slots[pl.ds(h * lower, lower), :] = total[:, pl.ds(h * width, width)].astype(slots.dtype)

    odd = lax.axis_index("lat") % 2 == 1
    for half in range(2):
        part = pl.ds(half * lanes, lanes)
        south = state[pl.ds(tile_row(0, half), width, stride=2 * ny), :]
        north = state[pl.ds(tile_row(ny - 1, half), width, stride=2 * ny), :]
        lat_even[:, part] = jnp.where(odd, south, north).astype(lat_even.dtype)
        lat_odd[:, part] = jnp.where(odd, north, south).astype(lat_odd.dtype)
    odd = lax.axis_index("span") == 1
    west, east = edges[pl.ds(0, ny), :], edges[pl.ds(ny, ny), :]
    lon_even[...] = jnp.where(odd, west, east).astype(lon_even.dtype)
    lon_odd[...] = jnp.where(odd, east, west).astype(lon_odd.dtype)


def dispatch(dest, slot, convect, state, group):
    ny, nx = dest.shape
    width, count = state.shape[0] // (ny * 2), ny * nx
    uppers, depth = 4, 4 * nx
    lower = count // uppers
    vmem = pl.BlockSpec(memory_space=pltpu.VMEM)
    kernel = lambda *refs: dispatch_kernel(ny, nx, *refs)
    shape = jax.ShapeDtypeStruct
    return pl.pallas_call(
        kernel,
        out_shape=(
            shape((count, width), jnp.bfloat16),
            shape((width, nx), jnp.bfloat16),
            shape((width, nx), jnp.bfloat16),
            shape((ny, width), jnp.bfloat16),
            shape((ny, width), jnp.bfloat16),
            shape((2, ny, nx // 2), jnp.int32),
            shape((group, width), jnp.int32),
        ),
        in_specs=[vmem, vmem, vmem, pl.BlockSpec(memory_space=pl.ANY)],
        out_specs=(vmem,) * 7,
        scratch_shapes=[
            pltpu.VMEM(state.shape, jnp.float32),
            pltpu.VMEM((2, depth, uppers * width), jnp.bfloat16),
            pltpu.VMEM((2, lower, depth), jnp.bfloat16),
            pltpu.VMEM((lower, uppers * width), jnp.float32),
            pltpu.VMEM((2 * ny, width), jnp.float32),
            pltpu.SemaphoreType.DMA,
        ],
        compiler_params=pltpu.CompilerParams(vmem_limit_bytes=63 * MIB),
        cost_estimate=pl.CostEstimate(
            flops=2 * count * count * width,
            bytes_accessed=6 * count * width,
            transcendentals=0,
        ),
        name="dispatch",
    )(dest, slot, convect, state)


def silu(v):
    half = 0.5 * v
    return half + half * jnp.tanh(half)


def network_kernel(capacity, filled, columns, recalled, w_in, w_mid, w_deep, w_out, tend, renewed):
    width = columns.shape[1]
    size, wide = PART, w_out.shape[1]
    parts = columns.shape[0] // size
    rows = [pl.ds(p * size, size) for p in range(parts)]
    values = [[columns[r, :], recalled[r, :]] for r in rows]
    waiting = []

    def settle():
        sums, kept = waiting.pop(0)
        kept.append(silu(sums).astype(jnp.bfloat16))

    for weights in (w_in, w_mid, w_deep):
        following = [[] for _ in rows]
        for p in range(parts):
            joined = jnp.concatenate(values[p], axis=1)
            for n in range(weights.shape[1] // wide):
                piece = weights[:, pl.ds(n * wide, wide)]
                sums = jnp.dot(joined, piece, preferred_element_type=jnp.float32)
                waiting.append((sums, following[p]))
                if len(waiting) > 1:
                    settle()
        values = following
    settle()
    owners = size // capacity
    place = lax.broadcasted_iota(jnp.int32, (capacity, width), 0)
    for p in range(parts):
        joined = jnp.concatenate(values[p], axis=1)
        result = jnp.dot(joined, w_out[...], preferred_element_type=jnp.float32)
        tend[rows[p], :] = result[:, :width].astype(tend.dtype)
        for o in range(owners):
            part = pl.ds(p * size + o * capacity, capacity)
            live = place < filled[pl.ds(p * owners + o, 1), :]
            update = result[o * capacity : (o + 1) * capacity, width:]
            old = recalled[part, :].astype(jnp.float32)
            renewed[part, :] = (old + jnp.where(live, update, 0.0)).astype(renewed.dtype)


def network(filled, columns, recalled, w_in, w_mid, w_deep, w_out):
    count, width = columns.shape
    capacity = count // filled.shape[0]
    rows = pl.BlockSpec((ROWS_MLP, width), lambda i: (i, 0))
    counts = pl.BlockSpec((ROWS_MLP // capacity, width), lambda i: (i, 0))
    whole = lambda w: pl.BlockSpec(w.shape, lambda i: (0, 0))
    kernel = lambda *refs: network_kernel(capacity, *refs)
    weights = (w_in, w_mid, w_deep, w_out)
    return pl.pallas_call(
        kernel,
        grid=(count // ROWS_MLP,),
        out_shape=(
            jax.ShapeDtypeStruct((count, width), jnp.bfloat16),
            jax.ShapeDtypeStruct((count, width), jnp.bfloat16),
        ),
        in_specs=[counts, rows, rows] + [whole(w) for w in weights],
        out_specs=(rows, rows),
        compiler_params=pltpu.CompilerParams(vmem_limit_bytes=VMEM_LIMIT),
        cost_estimate=pl.CostEstimate(
            flops=2 * count * sum(w.size for w in weights),
            bytes_accessed=8 * count * width + 2 * sum(w.size for w in weights),
            transcendentals=count * 3 * w_mid.shape[0],
        ),
        name="network",
    )(filled, columns, recalled, *weights)


def finish_kernel(
    ny,
    nx,
    target,
    tend,
    state_hbm,
    winds_hbm,
    lat_even,
    lat_odd,
    lon_even,
    lon_odd,
    out,
    state,
    winds,
    table,
    low,
    high,
    west,
    east,
    arrived,
):
    width = state.shape[0] // (ny * 2)
    lanes = nx // 2
    subs = ny // SUB
    levels = winds.shape[0] // (4 * ny)
    copies = [
        pltpu.make_async_copy(state_hbm, state, arrived.at[0]),
        pltpu.make_async_copy(winds_hbm, winds, arrived.at[1]),
    ]
    for copy in copies:
        copy.start()
    lower = table.shape[1]
    uppers = table.shape[0] // width
    for h in range(uppers):
        rows = tend[pl.ds(h * lower, lower), :].astype(jnp.float32)
        table[pl.ds(h * width, width), :] = rows.T.astype(table.dtype)
    odd = lax.axis_index("span") == 1
    evens, odds = lon_even[...].astype(jnp.float32), lon_odd[...].astype(jnp.float32)
    west[...] = jnp.where(odd, evens, odds)
    east[...] = jnp.where(odd, odds, evens)
    odd = lax.axis_index("lat") % 2 == 1
    for half in range(2):
        part = pl.ds(half * lanes, lanes)
        evens, odds = lat_even[:, part].astype(jnp.float32), lat_odd[:, part].astype(jnp.float32)
        low[half] = jnp.where(odd, evens, odds)
        high[half] = jnp.where(odd, odds, evens)

    shift, mask = log2(lower), lower - 1

    for y in range(ny):
        index = jnp.concatenate([target[half, pl.ds(y, 1), :] for half in range(2)], axis=1)
        candidates = jnp.dot(
            table[...], one_hot(index & mask, lower), preferred_element_type=jnp.float32
        )
        upper = jnp.broadcast_to(index >> shift, (width, nx))
        change = jnp.zeros((width, nx), jnp.float32)
        for h in range(uppers):
            change = jnp.where(upper == h, candidates[h * width : (h + 1) * width], change)
        for half in range(2):
            place = pl.ds(tile_row(y, half), width, stride=2 * ny)
            out[place, :] = change[:, half * lanes : (half + 1) * lanes]
    for copy in copies:
        copy.wait()

    lane = lax.broadcasted_iota(jnp.int32, (SUB, lanes), 1)
    line = lax.broadcasted_iota(jnp.int32, (SUB, lanes), 0)
    tiles = [(sub, half) for sub in range(subs) for half in range(2)]

    def block(ref, r, sub, half):
        start = pl.multiple_of(r * (2 * ny), 2 * ny) + (sub * 2 + half) * SUB
        return ref.at[pl.ds(start, SUB), :]

    @pl.loop(0, levels, unroll=4)
    def _(k):
        zonal = {t: block(winds, k, *t)[...] for t in tiles}
        meridional = {t: block(winds, levels + k, *t)[...] for t in tiles}
        for f in range(width // levels):
            r = f * levels + k
            s = {t: block(state, r, *t)[...] for t in tiles}
            first = pltpu.roll(west[...], width - r, axis=1)
            last = pltpu.roll(east[...], width - 1 - r, axis=1)
            up = {t: pltpu.roll(s[t], 1, axis=1) for t in tiles}
            down = {t: pltpu.roll(s[t], lanes - 1, axis=1) for t in tiles}
            rise = {t: pltpu.roll(s[t], 1, axis=0) for t in tiles}
            fall = {t: pltpu.roll(s[t], SUB - 1, axis=0) for t in tiles}
            for sub, half in tiles:
                t = (sub, half)
                edge = slice(sub * SUB, (sub + 1) * SUB)
                left = jnp.where(lane == 0, up[sub, 0] if half else first[edge], up[t])
                right = jnp.where(lane == lanes - 1, last[edge] if half else down[sub, 1], down[t])
                under = rise[sub - 1, half] if sub else low[half, pl.ds(r, 1), :]
                over = fall[sub + 1, half] if sub < subs - 1 else high[half, pl.ds(r, 1), :]
                below = jnp.where(line == 0, under, rise[t])
                above = jnp.where(line == SUB - 1, over, fall[t])
                place = block(out, r, *t)
                place[...] = place[...] + (
                    s[t]
                    - jnp.maximum(zonal[t], 0.0) * (s[t] - left)
                    - jnp.minimum(zonal[t], 0.0) * (right - s[t])
                    - jnp.maximum(meridional[t], 0.0) * (s[t] - below)
                    - jnp.minimum(meridional[t], 0.0) * (above - s[t])
                )


def finish(target, tend, state, winds, *edges):
    _, ny, lanes = target.shape
    nx = 2 * lanes
    count, width = tend.shape
    uppers = 8
    vmem = pl.BlockSpec(memory_space=pltpu.VMEM)
    hbm = pl.BlockSpec(memory_space=pl.ANY)
    kernel = lambda *refs: finish_kernel(ny, nx, *refs)
    return pl.pallas_call(
        kernel,
        out_shape=jax.ShapeDtypeStruct(state.shape, jnp.float32),
        in_specs=[vmem, vmem, hbm, hbm, vmem, vmem, vmem, vmem],
        out_specs=vmem,
        scratch_shapes=[
            pltpu.VMEM(state.shape, jnp.float32),
            pltpu.VMEM(winds.shape, jnp.float32),
            pltpu.VMEM((uppers * width, count // uppers), jnp.bfloat16),
            pltpu.VMEM((2, width, nx // 2), jnp.float32),
            pltpu.VMEM((2, width, nx // 2), jnp.float32),
            pltpu.VMEM((ny, width), jnp.float32),
            pltpu.VMEM((ny, width), jnp.float32),
            pltpu.SemaphoreType.DMA((2,)),
        ],
        compiler_params=pltpu.CompilerParams(vmem_limit_bytes=VMEM_LIMIT),
        cost_estimate=pl.CostEstimate(
            flops=2 * count * count * width,
            bytes_accessed=14 * count * width,
            transcendentals=0,
        ),
        name="finish",
    )(target, tend, state, winds, *edges)


def to_tiles(field):
    fields, levels, ny, nx = field.shape
    tiles = field.reshape(fields * levels, ny // SUB, SUB, 2, nx // 2)
    return tiles.transpose(0, 1, 3, 2, 4).reshape(fields * levels * ny * 2, nx // 2)


def from_tiles(tiles, shape):
    fields, levels, ny, nx = shape
    field = tiles.reshape(fields * levels, ny // SUB, 2, SUB, nx // 2)
    return field.transpose(0, 1, 3, 2, 4).reshape(shape)


def body(state, winds, memory, w_in, w_mid, w_deep, w_out, dest, slot, convect):
    group = lax.axis_size(GROUP_AXES)

    recalled = exchange(memory)
    flat_state, flat_winds = to_tiles(state), to_tiles(winds)
    columns, lat_even, lat_odd, lon_even, lon_odd, target, filled = dispatch(
        dest, slot, convect, flat_state, group
    )
    loop = ("lon", "span")
    lon_even = swapped(lon_even, loop, 0, True)
    lon_odd = swapped(lon_odd, loop, 1, True)
    lat_even = swapped(lat_even, "lat", 0, False)
    lat_odd = swapped(lat_odd, "lat", 1, False)
    edges = (lat_even, lat_odd, lon_even)
    columns, edges = lax.optimization_barrier((columns, edges))
    tend, renewed = network(filled, columns, recalled, w_in, w_mid, w_deep, w_out)
    new_memory = exchange(renewed)
    new_state = finish(target, tend, flat_state, flat_winds, *edges, lon_odd)
    return from_tiles(new_state, state.shape), new_memory


def solution(mesh):
    field = P(None, None, "lat", ("lon", "span"))
    slots = P(("lon", "lat", "span"), None)
    plane = P("lat", ("lon", "span"))
    in_specs = (field, field, slots, P(), P(), P(), P(), plane, plane, plane)
    return jax.shard_map(
        body, mesh=mesh, in_specs=in_specs, out_specs=(field, slots), check_vma=False
    )
```

time: 144 us -> 65.1 us (0.45); the launches traced: 141 us -> 64.6 us
  local copies, waits for them, and re-layouts: 55.5 us -> 1.58 us
  Pallas kernels: 0 us -> 31.1 us
  other arithmetic: 30.5 us -> 0 us
  matrix products: 17.1 us -> 0 us
  starting transfers between devices: 31.8 us -> 27.5 us
  waiting for transfers between devices: 5.76 us -> 3.67 us
    pallas_call x0 -> x3, Pallas kernels: none -> 31.1 us  [the longest x1 11.1 us: finish(): pl.pallas_call(kernel, out_shape=jax.ShapeDtypeStruct(state.shape, jnp.fl...]
    gather x2 -> x0, local copies, waits for them, and re-layouts: 27.2 us -> none  [the longest x1 15 us: place_rows(): picked = values[jnp.minimum(source_of, values.shape[0] - 1)]]
    dot_general x2 -> x0, matrix products: 17.1 us -> none  [the longest x1 9.61 us: column_mlp(): result = jnp.dot(third, w_out, preferred_element_type=jnp.float32)]
    scatter x1 -> x0, local copies, waits for them, and re-layouts: 15.5 us -> none  [body(): jnp.full((count,), count, jnp.int32).at[parked].set(positions, mode='drop')]
    select_n x4 -> x0, other arithmetic: 9.81 us -> none  [the longest x1 3.52 us: body(): new_memory = jnp.where(arrived_flags[:, None] > 0, renewed, memory)]
    convert_element_type x3 -> x0, other arithmetic: 7.71 us -> none  [the longest x1 3.54 us: advect(): padded(state.astype(jnp.bfloat16), ((('lon', 'span'), 3),), 1, True)]
    all_to_all x3 -> x2, waiting for transfers between devices: 5.75 us -> 0.01 us  [exchange(): lax.all_to_all(rows, GROUP_AXES, split_axis=0, concat_axis=0, tiled=True)]
    add x1 -> x0, other arithmetic: 5.73 us -> none  [body(): new_state = dynamics + change.T.reshape(fields, levels, rows_lat, rows_lon)]
  transfers between devices with their start and end apart: 7 -> 6, of which waited for: 2 -> 3; matrix products, arithmetic and copies ran while one was open for 41% -> 0% of each run, Pallas kernels for 0% -> 32%
where the time goes in v1:
time: 65.1 us; the launch traced here: 64.6 us
  Pallas kernels  31.1 us (48%)
  starting transfers between devices  27.5 us (42%)
  waiting for transfers between devices  3.67 us (6%)
  local copies, waits for them, and re-layouts  1.58 us (2%)
  between operations  0.72 us (1%)
    all_to_all x2, starting transfers between devices, exchange(): lax.all_to_all(rows, GROUP_AXES, split_axis=0, concat_axis=0, tiled=True)  17.1 us
    pallas_call x1, Pallas kernels, finish(): pl.pallas_call(kernel, out_shape=jax.ShapeDtypeStruct(state.shape, jnp.fl...  11.1 us
    pallas_call x1, Pallas kernels, network(): pl.pallas_call(kernel, grid=(count // ROWS_MLP,), out_shape=(jax.ShapeDty...  10.6 us
    ppermute x4, starting transfers between devices, swapped(): return lax.ppermute(edge, axis, pairs + [(j, i) for i, j in pairs])  10.4 us
    pallas_call x1, Pallas kernels, dispatch(): pl.pallas_call(kernel, out_shape=(shape((count, width), jnp.bfloat16), sh...  9.41 us
    ppermute x4, waiting for transfers between devices, swapped(): return lax.ppermute(edge, axis, pairs + [(j, i) for i, j in pairs])  3.66 us
    unnamed x11, local copies, waits for them, and re-layouts  1.58 us
  transfers between devices with their start and end apart: 6, of which 3 were waited for; matrix products, arithmetic and copies ran while one was open for 0% of the time, Pallas kernels for 32%

profile of v1, /device:TPU:2, one launch (start us, length us, event | category | flops | bytes accessed | tf_op | source)
XLA Modules:
  0.0 64.6 jit_solution(1402744103552218456)
XLA Ops:
  0.6 7.7 %all-to-all-start = ((bf16[32,128,128]{2,1,0:T(8,128)(2,1)}), bf16[32,128,128]{2,1,0:T(8,128)(2,1)}, u32[]{:S(2)}, u32[]{:S(2)}) async-start(bf16[32,128,128]{2,1,0:T(8,128)(2,1)} %bitcast.20), calls=%async_computation | async-start | bytes 2097152 | tf_op jit(solution)/shard_map/all_to_all | solution.py:23
  8.3 9.4 %dispatch.1 = (bf16[4096,128]{1,0:T(8,128)(2,1)}, bf16[128,256]{1,0:T(8,128)(2,1)}, bf16[128,256]{1,0:T(8,128)(2,1)}, bf16[16,128]{1,0:T(8,128)(2,1)}, bf16[16,1...) custom-call(s32[16,256]{1,0:T(8,128)} %refs_0_.1, s32[16,256]{1,0:T(8,128)} %refs_1_.1, ...), custom_call_target="tpu_custom_call" | custom-call | flops 4294967296 | bytes 3145728 | tf_op jit(solution)/shard_map/dispatch/pallas_call | solution.py:140
  17.7 0.4 collective-permute-start
  18.1 4.2 %collective-permute-start.1 = (bf16[128,256]{1,0:T(8,128)(2,1)}, bf16[128,256]{1,0:T(8,128)(2,1)S(1)}, u32[]{:S(2)}, u32[]{:S(2)}) collective-permute-start(bf16[128,256]{1,0:T(8,128)(2,1)} %get-tuple-element.19), channel_id=1, source_target_pairs={{2,4},{6,8},{10,12},{14,16},{18,20},{22,24},{26,28},{4,2},{8,6},{1... | collective-permute-start | bytes 196616 | tf_op jit(solution)/shard_map/ppermute | solution.py:19
  22.4 0.1 collective-permute-start.2
  22.5 1.4 %collective-permute-done.2.refs_6_ = bf16[16,128]{1,0:T(8,128)(2,1)S(1)} collective-permute-done((bf16[16,128]{1,0:T(8,128)(2,1)}, bf16[16,128]{1,0:T(8,128)(2,1)S(1)}, u32[]{:S(2)}, u32[]{:S(2)}) %collective-permute-start.2) | collective-permute-done | bytes 4128 | tf_op jit(solution)/shard_map/ppermute | solution.py:19
  23.8 0.0 copy-start.3
  23.8 0.0 collective-permute-done.refs_4_
  23.8 0.0 copy-start
  23.8 1.0 %collective-permute-done.1.refs_5_ = bf16[128,256]{1,0:T(8,128)(2,1)S(1)} collective-permute-done((bf16[128,256]{1,0:T(8,128)(2,1)}, bf16[128,256]{1,0:T(8,128)(2,1)S(1)}, u32[]{:S(2)}, u32[]{:S(2)}) %collective-permute-start.1) | collective-permute-done | bytes 65568 | tf_op jit(solution)/shard_map/ppermute | solution.py:19
  24.8 0.0 all-to-all-done
  24.8 10.6 %network.1 = (bf16[4096,128]{1,0:T(8,128)(2,1)}, bf16[4096,128]{1,0:T(8,128)(2,1)}) custom-call(s32[32,128]{1,0:T(8,128)} %get-tuple-element.16.refs_0_, bf16[4096,128]{1,0:T(8,128)(2,1)} %get-tuple-element.21.refs_1_, bf16[4096,128]{1,0:T(8,128)(2,1)} %bitcast.4.refs_2_, bf16[256,512]{1,0:T(8,128)(2,1)} %refs_3_.1, bf16[512,512]{1,0:T(8,128)(2,1)} %refs_4_.1, ...), custom_call_target="tpu_custom_call" | custom-call | flops 6442450944 | bytes 5767168 | tf_op jit(solution)/shard_map/network/pallas_call | solution.py:222
  35.4 0.0 copy-done.3
  35.4 0.0 copy-done
  35.4 0.0 copy-done.1
  35.4 0.0 copy-start.2
  35.4 9.5 %all-to-all-start.1 = ((bf16[32,128,128]{2,1,0:T(8,128)(2,1)}), bf16[32,128,128]{2,1,0:T(8,128)(2,1)S(1)}, u32[]{:S(2)}, u32[]{:S(2)}) async-start(bf16[32,128,128]{2,1,0:T(8,128)(2,1)} %bitcast.21), calls=%async_computation.1 | async-start | bytes 2097152 | tf_op jit(solution)/shard_map/all_to_all | solution.py:23
  44.9 0.0 copy-done.2
  44.9 5.7 %collective-permute-start.3 = (bf16[16,128]{1,0:T(8,128)(2,1)S(1)}, bf16[16,128]{1,0:T(8,128)(2,1)S(1)}, u32[]{:S(2)}, u32[]{:S(2)}) collective-permute-start(bf16[16,128]{1,0:T(8,128)(2,1)S(1)} %copy-done.2), channel_id=1, source_target_pairs={{1,32},{33,64},{65,96},{97,128},{129,160},{161,192},{193,224},{225... | collective-permute-start | bytes 12296 | tf_op jit(solution)/shard_map/ppermute | solution.py:19
  50.6 1.3 %collective-permute-done.3.refs_7_ = bf16[16,128]{1,0:T(8,128)(2,1)S(1)} collective-permute-done((bf16[16,128]{1,0:T(8,128)(2,1)S(1)}, bf16[16,128]{1,0:T(8,128)(2,1)S(1)}, u32[]{:S(2)}, u32[]{:S(2)}) %collective-permute-start.3) | collective-permute-done | bytes 4128 | tf_op jit(solution)/shard_map/ppermute | solution.py:19
  51.9 0.6 copy-done.4
  52.5 11.1 %finish.1 = f32[4096,128]{1,0:T(8,128)} custom-call(s32[2,16,128]{2,1,0:T(8,128)} %get-tuple-element.15.refs_0_, bf16[4096,128]{1,0:T(8,128)(2,1)} %get-tuple-element.22.refs_1_, f32[4096,128]{1,0:T(8,128)} %bitcast.23, f32[4096,128]{1,0:T(8,128)} %bitcast.24, bf16[128,256]{1,0:T(8,128)(2,1)} %copy-done, bf16[128,256]{1,0:T(8,128)(2,1)} %copy-done.1, ...), custom_call_target="tpu_custom_call" | custom-call | flops 4294967296 | bytes 7340032 | tf_op jit(solution)/shard_map/finish/pallas_call | solution.py:353
  63.6 0.0 all-to-all-done.1
  63.7 1.0 %copy.13 = bf16[4096,128]{1,0:T(8,128)(2,1)} copy(bf16[4096,128]{1,0:T(8,128)(2,1)S(1)} %bitcast.19) | data formatting | bytes 2097152
  (2 shorter events, 0.0 us)
Async XLA Ops:
  0.6 24.2 %all-to-all-start = ((bf16[32,128,128]{2,1,0:T(8,128)(2,1)}), bf16[32,128,128]{2,1,0:T(8,128)(2,1)}, u32[]{:S(2)}, u32[]{:S(2)}) async-start(bf16[32,128,128]{2,1,0:T(8,128)(2,1)} %bitcast.20), calls=%async_computation | async-start | bytes 2097152 | tf_op jit(solution)/shard_map/all_to_all | solution.py:23
  17.7 6.1 %collective-permute-start = (bf16[128,256]{1,0:T(8,128)(2,1)}, bf16[128,256]{1,0:T(8,128)(2,1)S(1)}, u32[]{:S(2)}, u32[]{:S(2)}) collective-permute-start(bf16[128,256]{1,0:T(8,128)(2,1)} %get-tuple-element.18), channel_id=1, source_target_pairs={{0,2},{4,6},{8,10},{12,14},{16,18},{20,22},{24,26},{28,30},{2,0},{... | collective-permute-start | bytes 196616 | tf_op jit(solution)/shard_map/ppermute | solution.py:19
  18.1 6.7 %collective-permute-start.1 = (bf16[128,256]{1,0:T(8,128)(2,1)}, bf16[128,256]{1,0:T(8,128)(2,1)S(1)}, u32[]{:S(2)}, u32[]{:S(2)}) collective-permute-start(bf16[128,256]{1,0:T(8,128)(2,1)} %get-tuple-element.19), channel_id=1, source_target_pairs={{2,4},{6,8},{10,12},{14,16},{18,20},{22,24},{26,28},{4,2},{8,6},{1... | collective-permute-start | bytes 196616 | tf_op jit(solution)/shard_map/ppermute | solution.py:19
  22.4 1.5 %collective-permute-start.2 = (bf16[16,128]{1,0:T(8,128)(2,1)}, bf16[16,128]{1,0:T(8,128)(2,1)S(1)}, u32[]{:S(2)}, u32[]{:S(2)}) collective-permute-start(bf16[16,128]{1,0:T(8,128)(2,1)} %get-tuple-element.20), channel_id=1, source_target_pairs={{0,1},{32,33},{64,65},{96,97},{128,129},{160,161},{192,193},{224,2... | collective-permute-start | bytes 12296 | tf_op jit(solution)/shard_map/ppermute | solution.py:19
  23.8 11.6 %copy-start.3 = (bf16[16,128]{1,0:T(8,128)(2,1)}, bf16[16,128]{1,0:T(8,128)(2,1)S(1)}, u32[]{:S(2)}) copy-start(bf16[16,128]{1,0:T(8,128)(2,1)S(1)} %collective-permute-done.2.refs_6_) | copy-start | bytes 12292
  23.8 11.6 %copy-start = (bf16[128,256]{1,0:T(8,128)(2,1)}, bf16[128,256]{1,0:T(8,128)(2,1)S(1)}, u32[]{:S(2)}) copy-start(bf16[128,256]{1,0:T(8,128)(2,1)S(1)} %collective-permute-done.refs_4_) | copy-start | bytes 196612
  24.8 10.6 %copy-start.1 = (bf16[128,256]{1,0:T(8,128)(2,1)}, bf16[128,256]{1,0:T(8,128)(2,1)S(1)}, u32[]{:S(2)}) copy-start(bf16[128,256]{1,0:T(8,128)(2,1)S(1)} %collective-permute-done.1.refs_5_) | copy-start | bytes 196612
  35.4 9.5 %copy-start.2 = (bf16[16,128]{1,0:T(8,128)(2,1)S(1)}, bf16[16,128]{1,0:T(8,128)(2,1)}, u32[]{:S(2)}) copy-start(bf16[16,128]{1,0:T(8,128)(2,1)} %get-tuple-element.26) | copy-start | bytes 12292
  35.4 28.2 %all-to-all-start.1 = ((bf16[32,128,128]{2,1,0:T(8,128)(2,1)}), bf16[32,128,128]{2,1,0:T(8,128)(2,1)S(1)}, u32[]{:S(2)}, u32[]{:S(2)}) async-start(bf16[32,128,128]{2,1,0:T(8,128)(2,1)} %bitcast.21), calls=%async_computation.1 | async-start | bytes 2097152 | tf_op jit(solution)/shard_map/all_to_all | solution.py:23
  44.9 7.0 %collective-permute-start.3 = (bf16[16,128]{1,0:T(8,128)(2,1)S(1)}, bf16[16,128]{1,0:T(8,128)(2,1)S(1)}, u32[]{:S(2)}, u32[]{:S(2)}) collective-permute-start(bf16[16,128]{1,0:T(8,128)(2,1)S(1)} %copy-done.2), channel_id=1, source_target_pairs={{1,32},{33,64},{65,96},{97,128},{129,160},{161,192},{193,224},{225... | collective-permute-start | bytes 12296 | tf_op jit(solution)/shard_map/ppermute | solution.py:19
  51.9 0.6 copy-start.4

commit v2 on v1

--- a/solution.py
+++ b/solution.py
@@ -168,14 +168,32 @@
     )(dest, slot, convect, state)
 
 
-def silu(v):
-    half = 0.5 * v
+def silu_of_half(half):
     return half + half * jnp.tanh(half)
 
 
-def network_kernel(capacity, filled, columns, recalled, w_in, w_mid, w_deep, w_out, tend, renewed):
+def network_kernel(
+    capacity,
+    filled,
+    columns,
+    recalled,
+    w_in,
+    w_mid,
+    w_deep,
+    w_out,
+    tend,
+    renewed,
+    half_in,
+    half_mid,
+    half_deep,
+):
+    @pl.when(pl.program_id(0) == 0)
+    def _():
+        for half, weights in ((half_in, w_in), (half_mid, w_mid), (half_deep, w_deep)):
+            half[...] = weights[...] * jnp.bfloat16(0.5)
+
     width = columns.shape[1]
-    size, wide = PART, w_out.shape[1]
+    size, wide = PART, w_in.shape[1]
     parts = columns.shape[0] // size
     rows = [pl.ds(p * size, size) for p in range(parts)]
     values = [[columns[r, :], recalled[r, :]] for r in rows]
@@ -183,9 +201,9 @@
 
     def settle():
         sums, kept = waiting.pop(0)
-        kept.append(silu(sums).astype(jnp.bfloat16))
-
-    for weights in (w_in, w_mid, w_deep):
+        kept.append(silu_of_half(sums).astype(jnp.bfloat16))
+
+    for weights in (half_in, half_mid, half_deep):
         following = [[] for _ in rows]
         for p in range(parts):
             joined = jnp.concatenate(values[p], axis=1)
@@ -228,6 +246,7 @@
         ),
         in_specs=[counts, rows, rows] + [whole(w) for w in weights],
         out_specs=(rows, rows),
+        scratch_shapes=[pltpu.VMEM(w.shape, w.dtype) for w in weights[:3]],
         compiler_params=pltpu.CompilerParams(vmem_limit_bytes=VMEM_LIMIT),
         cost_estimate=pl.CostEstimate(
             flops=2 * count * sum(w.size for w in weights),
@@ -242,52 +261,62 @@
     ny,
     nx,
     target,
-    tend,
+    tend_hbm,
     state_hbm,
     winds_hbm,
     lat_even,
     lat_odd,
     lon_even,
     lon_odd,
-    out,
+    out_hbm,
+    tend,
     state,
     winds,
     table,
     low,
     high,
-    west,
-    east,
+    moved,
+    flow,
     arrived,
+    left_over,
 ):
     width = state.shape[0] // (ny * 2)
     lanes = nx // 2
     subs = ny // SUB
     levels = winds.shape[0] // (4 * ny)
     copies = [
-        pltpu.make_async_copy(state_hbm, state, arrived.at[0]),
-        pltpu.make_async_copy(winds_hbm, winds, arrived.at[1]),
+        pltpu.make_async_copy(tend_hbm, tend, arrived.at[0]),
+        pltpu.make_async_copy(state_hbm, state, arrived.at[1]),
+        pltpu.make_async_copy(winds_hbm, winds, arrived.at[2]),
     ]
     for copy in copies:
         copy.start()
-    lower = table.shape[1]
-    uppers = table.shape[0] // width
-    for h in range(uppers):
-        rows = tend[pl.ds(h * lower, lower), :].astype(jnp.float32)
-        table[pl.ds(h * width, width), :] = rows.T.astype(table.dtype)
     odd = lax.axis_index("span") == 1
     evens, odds = lon_even[...].astype(jnp.float32), lon_odd[...].astype(jnp.float32)
-    west[...] = jnp.where(odd, evens, odds)
-    east[...] = jnp.where(odd, odds, evens)
+    west = jnp.where(odd, evens, odds)
+    east = jnp.where(odd, odds, evens)
     odd = lax.axis_index("lat") % 2 == 1
     for half in range(2):
         part = pl.ds(half * lanes, lanes)
         evens, odds = lat_even[:, part].astype(jnp.float32), lat_odd[:, part].astype(jnp.float32)
         low[half] = jnp.where(odd, evens, odds)
         high[half] = jnp.where(odd, odds, evens)
-
+    lower = table.shape[1]
+    uppers = table.shape[0] // width
     shift, mask = log2(lower), lower - 1
-
-    for y in range(ny):
+    copies[0].wait()
+    for h in range(uppers):
+        rows = tend[pl.ds(h * lower, lower), :].astype(jnp.float32)
+        table[pl.ds(h * width, width), :] = rows.T.astype(table.dtype)
+
+    lane = lax.broadcasted_iota(jnp.int32, (SUB, lanes), 1)
+    line = lax.broadcasted_iota(jnp.int32, (SUB, lanes), 0)
+    tiles = [(sub, half) for sub in range(subs) for half in range(2)]
+
+    def block(r, sub, half):
+        return pl.ds(r * (2 * ny) + (sub * 2 + half) * SUB, SUB)
+
+    def move(y):
         index = jnp.concatenate([target[half, pl.ds(y, 1), :] for half in range(2)], axis=1)
         candidates = jnp.dot(
             table[...], one_hot(index & mask, lower), preferred_element_type=jnp.float32
@@ -298,27 +327,16 @@
             change = jnp.where(upper == h, candidates[h * width : (h + 1) * width], change)
         for half in range(2):
             place = pl.ds(tile_row(y, half), width, stride=2 * ny)
-            out[place, :] = change[:, half * lanes : (half + 1) * lanes]
-    for copy in copies:
-        copy.wait()
-
-    lane = lax.broadcasted_iota(jnp.int32, (SUB, lanes), 1)
-    line = lax.broadcasted_iota(jnp.int32, (SUB, lanes), 0)
-    tiles = [(sub, half) for sub in range(subs) for half in range(2)]
-
-    def block(ref, r, sub, half):
-        start = pl.multiple_of(r * (2 * ny), 2 * ny) + (sub * 2 + half) * SUB
-        return ref.at[pl.ds(start, SUB), :]
-
-    @pl.loop(0, levels, unroll=4)
-    def _(k):
-        zonal = {t: block(winds, k, *t)[...] for t in tiles}
-        meridional = {t: block(winds, levels + k, *t)[...] for t in tiles}
+            moved[place, :] = change[:, half * lanes : (half + 1) * lanes]
+
+    def advect(k):
+        zonal = {t: winds[block(k, *t), :] for t in tiles}
+        meridional = {t: winds[block(levels + k, *t), :] for t in tiles}
         for f in range(width // levels):
             r = f * levels + k
-            s = {t: block(state, r, *t)[...] for t in tiles}
-            first = pltpu.roll(west[...], width - r, axis=1)
-            last = pltpu.roll(east[...], width - 1 - r, axis=1)
+            s = {t: state[block(r, *t), :] for t in tiles}
+            first = pltpu.roll(west, (width - r) % width, axis=1)
+            last = pltpu.roll(east, width - 1 - r, axis=1)
             up = {t: pltpu.roll(s[t], 1, axis=1) for t in tiles}
             down = {t: pltpu.roll(s[t], lanes - 1, axis=1) for t in tiles}
             rise = {t: pltpu.roll(s[t], 1, axis=0) for t in tiles}
@@ -332,14 +350,34 @@
                 over = fall[sub + 1, half] if sub < subs - 1 else high[half, pl.ds(r, 1), :]
                 below = jnp.where(line == 0, under, rise[t])
                 above = jnp.where(line == SUB - 1, over, fall[t])
-                place = block(out, r, *t)
-                place[...] = place[...] + (
+                flow[block(r, *t), :] = (
                     s[t]
                     - jnp.maximum(zonal[t], 0.0) * (s[t] - left)
                     - jnp.minimum(zonal[t], 0.0) * (right - s[t])
                     - jnp.maximum(meridional[t], 0.0) * (s[t] - below)
                     - jnp.minimum(meridional[t], 0.0) * (above - s[t])
                 )
+
+    ahead = 2
+    share = levels // (ny - ahead) + 1
+    for y in range(ny):
+        move(y)
+        if y == ahead - 1:
+            copies[1].wait()
+            copies[2].wait()
+        start = (y - ahead) * share
+        for k in range(max(start, 0), max(min(start + share, levels), 0)):
+            advect(k)
+    pieces = left_over.shape[0]
+    size = state.shape[0] // pieces
+    sends = []
+    for p in range(pieces):
+        rows = pl.ds(p * size, size)
+        flow[rows, :] = flow[rows, :] + moved[rows, :]
+        sends.append(pltpu.make_async_copy(flow.at[rows, :], out_hbm.at[rows, :], left_over.at[p]))
+        sends[-1].start()
+    for send in sends:
+        send.wait()
 
 
 def finish(target, tend, state, winds, *edges):
@@ -353,17 +391,19 @@
     return pl.pallas_call(
         kernel,
         out_shape=jax.ShapeDtypeStruct(state.shape, jnp.float32),
-        in_specs=[vmem, vmem, hbm, hbm, vmem, vmem, vmem, vmem],
-        out_specs=vmem,
+        in_specs=[vmem, hbm, hbm, hbm, vmem, vmem, vmem, vmem],
+        out_specs=hbm,
         scratch_shapes=[
+            pltpu.VMEM(tend.shape, tend.dtype),
             pltpu.VMEM(state.shape, jnp.float32),
             pltpu.VMEM(winds.shape, jnp.float32),
             pltpu.VMEM((uppers * width, count // uppers), jnp.bfloat16),
-            pltpu.VMEM((2, width, nx // 2), jnp.float32),
-            pltpu.VMEM((2, width, nx // 2), jnp.float32),
-            pltpu.VMEM((ny, width), jnp.float32),
-            pltpu.VMEM((ny, width), jnp.float32),
-            pltpu.SemaphoreType.DMA((2,)),
+            pltpu.VMEM((2, width, lanes), jnp.float32),
+            pltpu.VMEM((2, width, lanes), jnp.float32),
+            pltpu.VMEM(state.shape, jnp.float32),
+            pltpu.VMEM(state.shape, jnp.float32),
+            pltpu.SemaphoreType.DMA((3,)),
+            pltpu.SemaphoreType.DMA((4,)),
         ],
         compiler_params=pltpu.CompilerParams(vmem_limit_bytes=VMEM_LIMIT),
         cost_estimate=pl.CostEstimate(
@@ -400,9 +440,9 @@
     lon_odd = swapped(lon_odd, loop, 1, True)
     lat_even = swapped(lat_even, "lat", 0, False)
     lat_odd = swapped(lat_odd, "lat", 1, False)
+    tend, renewed = network(filled, columns, recalled, w_in, w_mid, w_deep, w_out)
     edges = (lat_even, lat_odd, lon_even)
-    columns, edges = lax.optimization_barrier((columns, edges))
-    tend, renewed = network(filled, columns, recalled, w_in, w_mid, w_deep, w_out)
+    renewed, edges = lax.optimization_barrier((renewed, edges))
     new_memory = exchange(renewed)
     new_state = finish(target, tend, flat_state, flat_winds, *edges, lon_odd)
     return from_tiles(new_state, state.shape), new_memory

time: 65.1 us -> 59.8 us (0.919)
  starting transfers between devices: 27.5 us -> 23.6 us
  Pallas kernels: 31.1 us -> 30.1 us
    all_to_all x2, starting transfers between devices: 17.1 us -> 13 us  [exchange(): lax.all_to_all(rows, GROUP_AXES, split_axis=0, concat_axis=0, tiled=True)]
    ppermute x4, waiting for transfers between devices: 3.66 us -> 1.34 us  [swapped(): return lax.ppermute(edge, axis, pairs + [(j, i) for i, j in pairs])]
    all_to_all x2, waiting for transfers between devices: 0.01 us -> 1.96 us  [exchange(): lax.all_to_all(rows, GROUP_AXES, split_axis=0, concat_axis=0, tiled=True)]
    pallas_call x1, Pallas kernels: 10.6 us -> 9.88 us  [network(): pl.pallas_call(kernel, grid=(count // ROWS_MLP,), out_shape=(jax.ShapeDty...]
  transfers between devices with their start and end apart: 6 -> 6, of which waited for: 3 -> 2; matrix products, arithmetic and copies ran while one was open for 0% -> 0% of each run, Pallas kernels for 32% -> 51%
where the time goes in v2:
time: 59.8 us; the launch traced here: 59.3 us
  Pallas kernels  30.1 us (50%)
  starting transfers between devices  23.6 us (39%)
  waiting for transfers between devices  3.29 us (6%)
  local copies, waits for them, and re-layouts  1.55 us (3%)
  between operations  0.74 us (1%)
    all_to_all x2, starting transfers between devices, exchange(): lax.all_to_all(rows, GROUP_AXES, split_axis=0, concat_axis=0, tiled=True)  13 us
    pallas_call x1, Pallas kernels, finish(): pl.pallas_call(kernel, out_shape=jax.ShapeDtypeStruct(state.shape, jnp.fl...  10.8 us
    ppermute x4, starting transfers between devices, swapped(): return lax.ppermute(edge, axis, pairs + [(j, i) for i, j in pairs])  10.7 us
    pallas_call x1, Pallas kernels, network(): pl.pallas_call(kernel, grid=(count // ROWS_MLP,), out_shape=(jax.ShapeDty...  9.88 us
    pallas_call x1, Pallas kernels, dispatch(): pl.pallas_call(kernel, out_shape=(shape((count, width), jnp.bfloat16), sh...  9.42 us
    all_to_all x2, waiting for transfers between devices, exchange(): lax.all_to_all(rows, GROUP_AXES, split_axis=0, concat_axis=0, tiled=True)  1.96 us
    unnamed x11, local copies, waits for them, and re-layouts  1.55 us
    ppermute x4, waiting for transfers between devices, swapped(): return lax.ppermute(edge, axis, pairs + [(j, i) for i, j in pairs])  1.34 us
  transfers between devices with their start and end apart: 6, of which 2 were waited for; matrix products, arithmetic and copies ran while one was open for 0% of the time, Pallas kernels for 51%

profile of v2, /device:TPU:2, one launch (start us, length us, event | category | flops | bytes accessed | tf_op | source)
XLA Modules:
  0.0 59.3 jit_solution(17385524953473048109)
XLA Ops:
  0.6 7.7 %all-to-all-start = ((bf16[32,128,128]{2,1,0:T(8,128)(2,1)}), bf16[32,128,128]{2,1,0:T(8,128)(2,1)}, u32[]{:S(2)}, u32[]{:S(2)}) async-start(bf16[32,128,128]{2,1,0:T(8,128)(2,1)} %bitcast.20), calls=%async_computation | async-start | bytes 2097152 | tf_op jit(solution)/shard_map/all_to_all | solution.py:23
  8.3 9.4 %dispatch.1 = (bf16[4096,128]{1,0:T(8,128)(2,1)}, bf16[128,256]{1,0:T(8,128)(2,1)}, bf16[128,256]{1,0:T(8,128)(2,1)}, bf16[16,128]{1,0:T(8,128)(2,1)}, bf16[16,1...) custom-call(s32[16,256]{1,0:T(8,128)} %refs_0_.1, s32[16,256]{1,0:T(8,128)} %refs_1_.1, ...), custom_call_target="tpu_custom_call" | custom-call | flops 4294967296 | bytes 3145728 | tf_op jit(solution)/shard_map/dispatch/pallas_call | solution.py:140
  17.7 0.2 collective-permute-start.2
  18.0 0.4 collective-permute-start
  18.3 4.2 %collective-permute-start.1 = (bf16[128,256]{1,0:T(8,128)(2,1)}, bf16[128,256]{1,0:T(8,128)(2,1)S(1)}, u32[]{:S(2)}, u32[]{:S(2)}) collective-permute-start(bf16[128,256]{1,0:T(8,128)(2,1)} %get-tuple-element.21), channel_id=1, source_target_pairs={{2,4},{6,8},{10,12},{14,16},{18,20},{22,24},{26,28},{4,2},{8,6},{1... | collective-permute-start | bytes 196616 | tf_op jit(solution)/shard_map/ppermute | solution.py:19
  22.5 2.0 %all-to-all-done = bf16[32,128,128]{2,1,0:T(8,128)(2,1)} async-done(((bf16[32,128,128]{2,1,0:T(8,128)(2,1)}), bf16[32,128,128]{2,1,0:T(8,128)(2,1)}, u32[]{:S(2)}, u32[]{:S(2)}) %all-to-all-start) | async-done | bytes 1048608 | tf_op jit(solution)/shard_map/all_to_all | solution.py:23
  24.5 9.9 %network.1 = (bf16[4096,128]{1,0:T(8,128)(2,1)}, bf16[4096,128]{1,0:T(8,128)(2,1)}) custom-call(s32[32,128]{1,0:T(8,128)} %get-tuple-element.16.refs_0_, bf16[4096,128]{1,0:T(8,128)(2,1)} %get-tuple-element.17.refs_1_, bf16[4096,128]{1,0:T(8,128)(2,1)} %bitcast.4.refs_2_, bf16[256,512]{1,0:T(8,128)(2,1)} %refs_3_.1, bf16[512,512]{1,0:T(8,128)(2,1)} %refs_4_.1, ...), custom_call_target="tpu_custom_call" | custom-call | flops 6442450944 | bytes 5767168 | tf_op jit(solution)/shard_map/network/pallas_call | solution.py:240
  34.4 0.0 collective-permute-done.2.refs_6_
  34.4 0.0 copy-start.2
  34.4 0.0 collective-permute-done.refs_4_
  34.4 0.0 copy-start
  34.4 0.0 collective-permute-done.1.refs_5_
  34.4 0.0 copy-start.1
  34.4 5.3 %all-to-all-start.1 = ((bf16[32,128,128]{2,1,0:T(8,128)(2,1)}), bf16[32,128,128]{2,1,0:T(8,128)(2,1)S(1)}, u32[]{:S(2)}, u32[]{:S(2)}) async-start(bf16[32,128,128]{2,1,0:T(8,128)(2,1)} %bitcast.21), calls=%async_computation.1 | async-start | bytes 2097152 | tf_op jit(solution)/shard_map/all_to_all | solution.py:23
  39.7 0.0 copy-done.3
  39.7 5.9 %collective-permute-start.3 = (bf16[16,128]{1,0:T(8,128)(2,1)S(1)}, bf16[16,128]{1,0:T(8,128)(2,1)S(1)}, u32[]{:S(2)}, u32[]{:S(2)}) collective-permute-start(bf16[16,128]{1,0:T(8,128)(2,1)S(1)} %copy-done.3), channel_id=1, source_target_pairs={{1,32},{33,64},{65,96},{97,128},{129,160},{161,192},{193,224},{225... | collective-permute-start | bytes 12296 | tf_op jit(solution)/shard_map/ppermute | solution.py:19
  45.6 1.3 %collective-permute-done.3.refs_7_ = bf16[16,128]{1,0:T(8,128)(2,1)S(1)} collective-permute-done((bf16[16,128]{1,0:T(8,128)(2,1)S(1)}, bf16[16,128]{1,0:T(8,128)(2,1)S(1)}, u32[]{:S(2)}, u32[]{:S(2)}) %collective-permute-start.3) | collective-permute-done | bytes 4128 | tf_op jit(solution)/shard_map/ppermute | solution.py:19
  46.9 0.0 copy-done.2
  46.9 0.0 copy-done
  46.9 0.0 copy-done.1
  46.9 0.6 copy-done.4
  47.5 10.8 %finish.1 = f32[4096,128]{1,0:T(8,128)} custom-call(s32[2,16,128]{2,1,0:T(8,128)} %get-tuple-element.15.refs_0_, bf16[4096,128]{1,0:T(8,128)(2,1)} %get-tuple-element.18.refs_1_, f32[4096,128]{1,0:T(8,128)} %bitcast.23, f32[4096,128]{1,0:T(8,128)} %bitcast.24, bf16[128,256]{1,0:T(8,128)(2,1)} %copy-done, bf16[128,256]{1,0:T(8,128)(2,1)} %copy-done.1, ...), custom_call_target="tpu_custom_call" | custom-call | flops 4294967296 | bytes 7340032 | tf_op jit(solution)/shard_map/finish/pallas_call | solution.py:391
  58.3 0.0 all-to-all-done.1
  58.3 1.0 %copy.13 = bf16[4096,128]{1,0:T(8,128)(2,1)} copy(bf16[4096,128]{1,0:T(8,128)(2,1)S(1)} %bitcast.19) | data formatting | bytes 2097152
  (2 shorter events, 0.0 us)
Async XLA Ops:
  0.6 23.9 %all-to-all-start = ((bf16[32,128,128]{2,1,0:T(8,128)(2,1)}), bf16[32,128,128]{2,1,0:T(8,128)(2,1)}, u32[]{:S(2)}, u32[]{:S(2)}) async-start(bf16[32,128,128]{2,1,0:T(8,128)(2,1)} %bitcast.20), calls=%async_computation | async-start | bytes 2097152 | tf_op jit(solution)/shard_map/all_to_all | solution.py:23
  17.7 16.6 %collective-permute-start.2 = (bf16[16,128]{1,0:T(8,128)(2,1)}, bf16[16,128]{1,0:T(8,128)(2,1)S(1)}, u32[]{:S(2)}, u32[]{:S(2)}) collective-permute-start(bf16[16,128]{1,0:T(8,128)(2,1)} %get-tuple-element.22), channel_id=1, source_target_pairs={{0,1},{32,33},{64,65},{96,97},{128,129},{160,161},{192,193},{224,2... | collective-permute-start | bytes 12296 | tf_op jit(solution)/shard_map/ppermute | solution.py:19
  18.0 16.4 %collective-permute-start = (bf16[128,256]{1,0:T(8,128)(2,1)}, bf16[128,256]{1,0:T(8,128)(2,1)S(1)}, u32[]{:S(2)}, u32[]{:S(2)}) collective-permute-start(bf16[128,256]{1,0:T(8,128)(2,1)} %get-tuple-element.20), channel_id=1, source_target_pairs={{0,2},{4,6},{8,10},{12,14},{16,18},{20,22},{24,26},{28,30},{2,0},{... | collective-permute-start | bytes 196616 | tf_op jit(solution)/shard_map/ppermute | solution.py:19
  18.3 16.1 %collective-permute-start.1 = (bf16[128,256]{1,0:T(8,128)(2,1)}, bf16[128,256]{1,0:T(8,128)(2,1)S(1)}, u32[]{:S(2)}, u32[]{:S(2)}) collective-permute-start(bf16[128,256]{1,0:T(8,128)(2,1)} %get-tuple-element.21), channel_id=1, source_target_pairs={{2,4},{6,8},{10,12},{14,16},{18,20},{22,24},{26,28},{4,2},{8,6},{1... | collective-permute-start | bytes 196616 | tf_op jit(solution)/shard_map/ppermute | solution.py:19
  34.4 5.3 %copy-start.3 = (bf16[16,128]{1,0:T(8,128)(2,1)S(1)}, bf16[16,128]{1,0:T(8,128)(2,1)}, u32[]{:S(2)}) copy-start(bf16[16,128]{1,0:T(8,128)(2,1)} %get-tuple-element.26) | copy-start | bytes 12292
  34.4 12.5 %copy-start.2 = (bf16[16,128]{1,0:T(8,128)(2,1)}, bf16[16,128]{1,0:T(8,128)(2,1)S(1)}, u32[]{:S(2)}) copy-start(bf16[16,128]{1,0:T(8,128)(2,1)S(1)} %collective-permute-done.2.refs_6_) | copy-start | bytes 12292
  34.4 12.5 %copy-start = (bf16[128,256]{1,0:T(8,128)(2,1)}, bf16[128,256]{1,0:T(8,128)(2,1)S(1)}, u32[]{:S(2)}) copy-start(bf16[128,256]{1,0:T(8,128)(2,1)S(1)} %collective-permute-done.refs_4_) | copy-start | bytes 196612
  34.4 12.5 %copy-start.1 = (bf16[128,256]{1,0:T(8,128)(2,1)}, bf16[128,256]{1,0:T(8,128)(2,1)S(1)}, u32[]{:S(2)}) copy-start(bf16[128,256]{1,0:T(8,128)(2,1)S(1)} %collective-permute-done.1.refs_5_) | copy-start | bytes 196612
  34.4 23.9 %all-to-all-start.1 = ((bf16[32,128,128]{2,1,0:T(8,128)(2,1)}), bf16[32,128,128]{2,1,0:T(8,128)(2,1)S(1)}, u32[]{:S(2)}, u32[]{:S(2)}) async-start(bf16[32,128,128]{2,1,0:T(8,128)(2,1)} %bitcast.21), calls=%async_computation.1 | async-start | bytes 2097152 | tf_op jit(solution)/shard_map/all_to_all | solution.py:23
  39.7 7.2 %collective-permute-start.3 = (bf16[16,128]{1,0:T(8,128)(2,1)S(1)}, bf16[16,128]{1,0:T(8,128)(2,1)S(1)}, u32[]{:S(2)}, u32[]{:S(2)}) collective-permute-start(bf16[16,128]{1,0:T(8,128)(2,1)S(1)} %copy-done.3), channel_id=1, source_target_pairs={{1,32},{33,64},{65,96},{97,128},{129,160},{161,192},{193,224},{225... | collective-permute-start | bytes 12296 | tf_op jit(solution)/shard_map/ppermute | solution.py:19
  46.9 0.6 copy-start.4

commit v3 on v2

--- a/solution.py
+++ b/solution.py
@@ -28,8 +28,15 @@
 
 
 def one_hot(index, size):
-    place = lax.broadcasted_iota(jnp.int32, (size, index.shape[1]), 0)
-    return (place == index).astype(jnp.bfloat16)
+    lanes = index.shape[1]
+    step = 2 * SUB
+    index = jnp.broadcast_to(index, (step, lanes)).astype(jnp.int16)
+    place = lax.broadcasted_iota(jnp.int32, (step, lanes), 0).astype(jnp.int16)
+    one, zero = jnp.ones((step, lanes), jnp.bfloat16), jnp.zeros((step, lanes), jnp.bfloat16)
+    blocks = [
+        jnp.where(index == place + jnp.int16(start), one, zero) for start in range(0, size, step)
+    ]
+    return jnp.concatenate(blocks, axis=0)
 
 
 def log2(size):
@@ -86,7 +93,7 @@
         for line in range(lines):
             y = g * lines + line
             choice[b, :, pl.ds(line * nx, nx)] = one_hot(goal[y : y + 1] & mask, lower)
-            upper = jnp.broadcast_to(goals[:, y : y + 1] >> shift, (nx, width))
+            upper = jnp.broadcast_to(goals[:, y : y + 1] >> shift, (nx, width)).astype(jnp.int16)
             for half in range(2):
                 part = slice(half * lanes, (half + 1) * lanes)
                 values = state[pl.ds(tile_row(y, half), width, stride=2 * ny), :].T
@@ -284,6 +291,7 @@
     lanes = nx // 2
     subs = ny // SUB
     levels = winds.shape[0] // (4 * ny)
+    count = ny * nx
     copies = [
         pltpu.make_async_copy(tend_hbm, tend, arrived.at[0]),
         pltpu.make_async_copy(state_hbm, state, arrived.at[1]),
@@ -318,13 +326,15 @@
 
     def move(y):
         index = jnp.concatenate([target[half, pl.ds(y, 1), :] for half in range(2)], axis=1)
+        wanted = jnp.where(index == count, -1, index & mask)
         candidates = jnp.dot(
-            table[...], one_hot(index & mask, lower), preferred_element_type=jnp.float32
-        )
-        upper = jnp.broadcast_to(index >> shift, (width, nx))
-        change = jnp.zeros((width, nx), jnp.float32)
-        for h in range(uppers):
-            change = jnp.where(upper == h, candidates[h * width : (h + 1) * width], change)
+            table[...], one_hot(wanted, lower), preferred_element_type=jnp.float32
+        ).reshape(uppers, width // SUB, SUB, nx)
+        upper = jnp.broadcast_to(index >> shift, (SUB, nx))
+        change = candidates[0]
+        for h in range(1, uppers):
+            change = jnp.where((upper == h)[None], candidates[h], change)
+        change = change.reshape(width, nx)
         for half in range(2):
             place = pl.ds(tile_row(y, half), width, stride=2 * ny)
             moved[place, :] = change[:, half * lanes : (half + 1) * lanes]

time: 59.8 us -> 59.6 us (level)
  transfers between devices with their start and end apart: 6 -> 6, of which waited for: 2 -> 2; matrix products, arithmetic and copies ran while one was open for 0% -> 0% of each run, Pallas kernels for 51% -> 50%
where the time goes in v3:
time: 59.6 us; the launch traced here: 59.2 us
  Pallas kernels  29.7 us (50%)
  starting transfers between devices  23.6 us (40%)
  waiting for transfers between devices  3.55 us (6%)
  local copies, waits for them, and re-layouts  1.55 us (3%)
  between operations  0.74 us (1%)
    all_to_all x2, starting transfers between devices, exchange(): lax.all_to_all(rows, GROUP_AXES, split_axis=0, concat_axis=0, tiled=True)  13 us
    pallas_call x1, Pallas kernels, finish(): pl.pallas_call(kernel, out_shape=jax.ShapeDtypeStruct(state.shape, jnp.fl...  10.7 us
    ppermute x4, starting transfers between devices, swapped(): return lax.ppermute(edge, axis, pairs + [(j, i) for i, j in pairs])  10.7 us
    pallas_call x1, Pallas kernels, network(): pl.pallas_call(kernel, grid=(count // ROWS_MLP,), out_shape=(jax.ShapeDty...  9.88 us
    pallas_call x1, Pallas kernels, dispatch(): pl.pallas_call(kernel, out_shape=(shape((count, width), jnp.bfloat16), sh...  9.16 us
    all_to_all x2, waiting for transfers between devices, exchange(): lax.all_to_all(rows, GROUP_AXES, split_axis=0, concat_axis=0, tiled=True)  2.21 us
    unnamed x11, local copies, waits for them, and re-layouts  1.55 us
    ppermute x4, waiting for transfers between devices, swapped(): return lax.ppermute(edge, axis, pairs + [(j, i) for i, j in pairs])  1.34 us
  transfers between devices with their start and end apart: 6, of which 2 were waited for; matrix products, arithmetic and copies ran while one was open for 0% of the time, Pallas kernels for 50%

profile of v3, /device:TPU:2, one launch (start us, length us, event | category | flops | bytes accessed | tf_op | source)
XLA Modules:
  0.0 59.2 jit_solution(13389806810433083100)
XLA Ops:
  0.6 7.7 %all-to-all-start = ((bf16[32,128,128]{2,1,0:T(8,128)(2,1)}), bf16[32,128,128]{2,1,0:T(8,128)(2,1)}, u32[]{:S(2)}, u32[]{:S(2)}) async-start(bf16[32,128,128]{2,1,0:T(8,128)(2,1)} %bitcast.20), calls=%async_computation | async-start | bytes 2097152 | tf_op jit(solution)/shard_map/all_to_all | solution.py:23
  8.3 9.2 %dispatch.1 = (bf16[4096,128]{1,0:T(8,128)(2,1)}, bf16[128,256]{1,0:T(8,128)(2,1)}, bf16[128,256]{1,0:T(8,128)(2,1)}, bf16[16,128]{1,0:T(8,128)(2,1)}, bf16[16,1...) custom-call(s32[16,256]{1,0:T(8,128)} %refs_0_.1, s32[16,256]{1,0:T(8,128)} %refs_1_.1, ...), custom_call_target="tpu_custom_call" | custom-call | flops 4294967296 | bytes 3145728 | tf_op jit(solution)/shard_map/dispatch/pallas_call | solution.py:147
  17.5 0.2 collective-permute-start.2
  17.7 0.4 collective-permute-start
  18.1 4.2 %collective-permute-start.1 = (bf16[128,256]{1,0:T(8,128)(2,1)}, bf16[128,256]{1,0:T(8,128)(2,1)S(1)}, u32[]{:S(2)}, u32[]{:S(2)}) collective-permute-start(bf16[128,256]{1,0:T(8,128)(2,1)} %get-tuple-element.21), channel_id=1, source_target_pairs={{2,4},{6,8},{10,12},{14,16},{18,20},{22,24},{26,28},{4,2},{8,6},{1... | collective-permute-start | bytes 196616 | tf_op jit(solution)/shard_map/ppermute | solution.py:19
  22.3 2.2 %all-to-all-done = bf16[32,128,128]{2,1,0:T(8,128)(2,1)} async-done(((bf16[32,128,128]{2,1,0:T(8,128)(2,1)}), bf16[32,128,128]{2,1,0:T(8,128)(2,1)}, u32[]{:S(2)}, u32[]{:S(2)}) %all-to-all-start) | async-done | bytes 1048608 | tf_op jit(solution)/shard_map/all_to_all | solution.py:23
  24.5 9.9 %network.1 = (bf16[4096,128]{1,0:T(8,128)(2,1)}, bf16[4096,128]{1,0:T(8,128)(2,1)}) custom-call(s32[32,128]{1,0:T(8,128)} %get-tuple-element.16.refs_0_, bf16[4096,128]{1,0:T(8,128)(2,1)} %get-tuple-element.17.refs_1_, bf16[4096,128]{1,0:T(8,128)(2,1)} %bitcast.4.refs_2_, bf16[256,512]{1,0:T(8,128)(2,1)} %refs_3_.1, bf16[512,512]{1,0:T(8,128)(2,1)} %refs_4_.1, ...), custom_call_target="tpu_custom_call" | custom-call | flops 6442450944 | bytes 5767168 | tf_op jit(solution)/shard_map/network/pallas_call | solution.py:247
  34.4 0.0 collective-permute-done.2.refs_6_
  34.4 0.0 copy-start.2
  34.4 0.0 collective-permute-done.refs_4_
  34.4 0.0 copy-start
  34.4 0.0 collective-permute-done.1.refs_5_
  34.4 0.0 copy-start.1
  34.4 5.3 %all-to-all-start.1 = ((bf16[32,128,128]{2,1,0:T(8,128)(2,1)}), bf16[32,128,128]{2,1,0:T(8,128)(2,1)S(1)}, u32[]{:S(2)}, u32[]{:S(2)}) async-start(bf16[32,128,128]{2,1,0:T(8,128)(2,1)} %bitcast.21), calls=%async_computation.1 | async-start | bytes 2097152 | tf_op jit(solution)/shard_map/all_to_all | solution.py:23
  39.7 0.0 copy-done.3
  39.7 5.9 %collective-permute-start.3 = (bf16[16,128]{1,0:T(8,128)(2,1)S(1)}, bf16[16,128]{1,0:T(8,128)(2,1)S(1)}, u32[]{:S(2)}, u32[]{:S(2)}) collective-permute-start(bf16[16,128]{1,0:T(8,128)(2,1)S(1)} %copy-done.3), channel_id=1, source_target_pairs={{1,32},{33,64},{65,96},{97,128},{129,160},{161,192},{193,224},{225... | collective-permute-start | bytes 12296 | tf_op jit(solution)/shard_map/ppermute | solution.py:19
  45.6 1.3 %collective-permute-done.3.refs_7_ = bf16[16,128]{1,0:T(8,128)(2,1)S(1)} collective-permute-done((bf16[16,128]{1,0:T(8,128)(2,1)S(1)}, bf16[16,128]{1,0:T(8,128)(2,1)S(1)}, u32[]{:S(2)}, u32[]{:S(2)}) %collective-permute-start.3) | collective-permute-done | bytes 4128 | tf_op jit(solution)/shard_map/ppermute | solution.py:19
  46.9 0.0 copy-done.2
  46.9 0.0 copy-done
  46.9 0.0 copy-done.1
  46.9 0.6 copy-done.4
  47.5 10.7 %finish.1 = f32[4096,128]{1,0:T(8,128)} custom-call(s32[2,16,128]{2,1,0:T(8,128)} %get-tuple-element.15.refs_0_, bf16[4096,128]{1,0:T(8,128)(2,1)} %get-tuple-element.18.refs_1_, f32[4096,128]{1,0:T(8,128)} %bitcast.23, f32[4096,128]{1,0:T(8,128)} %bitcast.24, bf16[128,256]{1,0:T(8,128)(2,1)} %copy-done, bf16[128,256]{1,0:T(8,128)(2,1)} %copy-done.1, ...), custom_call_target="tpu_custom_call" | custom-call | flops 4294967296 | bytes 7340032 | tf_op jit(solution)/shard_map/finish/pallas_call | solution.py:401
  58.2 0.0 all-to-all-done.1
  58.2 1.0 %copy.13 = bf16[4096,128]{1,0:T(8,128)(2,1)} copy(bf16[4096,128]{1,0:T(8,128)(2,1)S(1)} %bitcast.19) | data formatting | bytes 2097152
  (2 shorter events, 0.0 us)
Async XLA Ops:
  0.6 23.9 %all-to-all-start = ((bf16[32,128,128]{2,1,0:T(8,128)(2,1)}), bf16[32,128,128]{2,1,0:T(8,128)(2,1)}, u32[]{:S(2)}, u32[]{:S(2)}) async-start(bf16[32,128,128]{2,1,0:T(8,128)(2,1)} %bitcast.20), calls=%async_computation | async-start | bytes 2097152 | tf_op jit(solution)/shard_map/all_to_all | solution.py:23
  17.5 16.9 %collective-permute-start.2 = (bf16[16,128]{1,0:T(8,128)(2,1)}, bf16[16,128]{1,0:T(8,128)(2,1)S(1)}, u32[]{:S(2)}, u32[]{:S(2)}) collective-permute-start(bf16[16,128]{1,0:T(8,128)(2,1)} %get-tuple-element.22), channel_id=1, source_target_pairs={{0,1},{32,33},{64,65},{96,97},{128,129},{160,161},{192,193},{224,2... | collective-permute-start | bytes 12296 | tf_op jit(solution)/shard_map/ppermute | solution.py:19
  17.7 16.7 %collective-permute-start = (bf16[128,256]{1,0:T(8,128)(2,1)}, bf16[128,256]{1,0:T(8,128)(2,1)S(1)}, u32[]{:S(2)}, u32[]{:S(2)}) collective-permute-start(bf16[128,256]{1,0:T(8,128)(2,1)} %get-tuple-element.20), channel_id=1, source_target_pairs={{0,2},{4,6},{8,10},{12,14},{16,18},{20,22},{24,26},{28,30},{2,0},{... | collective-permute-start | bytes 196616 | tf_op jit(solution)/shard_map/ppermute | solution.py:19
  18.1 16.3 %collective-permute-start.1 = (bf16[128,256]{1,0:T(8,128)(2,1)}, bf16[128,256]{1,0:T(8,128)(2,1)S(1)}, u32[]{:S(2)}, u32[]{:S(2)}) collective-permute-start(bf16[128,256]{1,0:T(8,128)(2,1)} %get-tuple-element.21), channel_id=1, source_target_pairs={{2,4},{6,8},{10,12},{14,16},{18,20},{22,24},{26,28},{4,2},{8,6},{1... | collective-permute-start | bytes 196616 | tf_op jit(solution)/shard_map/ppermute | solution.py:19
  34.4 5.3 %copy-start.3 = (bf16[16,128]{1,0:T(8,128)(2,1)S(1)}, bf16[16,128]{1,0:T(8,128)(2,1)}, u32[]{:S(2)}) copy-start(bf16[16,128]{1,0:T(8,128)(2,1)} %get-tuple-element.26) | copy-start | bytes 12292
  34.4 12.5 %copy-start.2 = (bf16[16,128]{1,0:T(8,128)(2,1)}, bf16[16,128]{1,0:T(8,128)(2,1)S(1)}, u32[]{:S(2)}) copy-start(bf16[16,128]{1,0:T(8,128)(2,1)S(1)} %collective-permute-done.2.refs_6_) | copy-start | bytes 12292
  34.4 12.5 %copy-start = (bf16[128,256]{1,0:T(8,128)(2,1)}, bf16[128,256]{1,0:T(8,128)(2,1)S(1)}, u32[]{:S(2)}) copy-start(bf16[128,256]{1,0:T(8,128)(2,1)S(1)} %collective-permute-done.refs_4_) | copy-start | bytes 196612
  34.4 12.5 %copy-start.1 = (bf16[128,256]{1,0:T(8,128)(2,1)}, bf16[128,256]{1,0:T(8,128)(2,1)S(1)}, u32[]{:S(2)}) copy-start(bf16[128,256]{1,0:T(8,128)(2,1)S(1)} %collective-permute-done.1.refs_5_) | copy-start | bytes 196612
  34.4 23.8 %all-to-all-start.1 = ((bf16[32,128,128]{2,1,0:T(8,128)(2,1)}), bf16[32,128,128]{2,1,0:T(8,128)(2,1)S(1)}, u32[]{:S(2)}, u32[]{:S(2)}) async-start(bf16[32,128,128]{2,1,0:T(8,128)(2,1)} %bitcast.21), calls=%async_computation.1 | async-start | bytes 2097152 | tf_op jit(solution)/shard_map/all_to_all | solution.py:23
  39.7 7.2 %collective-permute-start.3 = (bf16[16,128]{1,0:T(8,128)(2,1)S(1)}, bf16[16,128]{1,0:T(8,128)(2,1)S(1)}, u32[]{:S(2)}, u32[]{:S(2)}) collective-permute-start(bf16[16,128]{1,0:T(8,128)(2,1)S(1)} %copy-done.3), channel_id=1, source_target_pairs={{1,32},{33,64},{65,96},{97,128},{129,160},{161,192},{193,224},{225... | collective-permute-start | bytes 12296 | tf_op jit(solution)/shard_map/ppermute | solution.py:19
  46.9 0.6 copy-start.4

commit v4 on v3

--- a/solution.py
+++ b/solution.py
@@ -43,6 +43,41 @@
     return size.bit_length() - 1
 
 
+def advect_level(ny, nx, state, winds, flow, k):
+    lanes, subs = nx // 2, ny // SUB
+    levels = winds.shape[0] // (4 * ny)
+    lane = lax.broadcasted_iota(jnp.int32, (SUB, lanes), 1)
+    line = lax.broadcasted_iota(jnp.int32, (SUB, lanes), 0)
+    tiles = [(sub, half) for sub in range(subs) for half in range(2)]
+
+    def block(r, sub, half):
+        return pl.ds(r * (2 * ny) + (sub * 2 + half) * SUB, SUB)
+
+    zonal = {t: winds[block(k, *t), :] for t in tiles}
+    meridional = {t: winds[block(levels + k, *t), :] for t in tiles}
+    for r in range(k, state.shape[0] // (2 * ny), levels):
+        s = {t: state[block(r, *t), :] for t in tiles}
+        up = {t: pltpu.roll(s[t], 1, axis=1) for t in tiles}
+        down = {t: pltpu.roll(s[t], lanes - 1, axis=1) for t in tiles}
+        rise = {t: pltpu.roll(s[t], 1, axis=0) for t in tiles}
+        fall = {t: pltpu.roll(s[t], SUB - 1, axis=0) for t in tiles}
+        for sub, half in tiles:
+            t = (sub, half)
+            left = jnp.where(lane == 0, up[sub, 0] if half else 0.0, up[t])
+            right = jnp.where(lane == lanes - 1, 0.0 if half else down[sub, 1], down[t])
+            below = jnp.where(line == 0, rise[sub - 1, half] if sub else 0.0, rise[t])
+            above = jnp.where(
+                line == SUB - 1, fall[sub + 1, half] if sub < subs - 1 else 0.0, fall[t]
+            )
+            flow[block(r, *t), :] = (
+                s[t]
+                - jnp.maximum(zonal[t], 0.0) * (s[t] - left)
+                - jnp.minimum(zonal[t], 0.0) * (right - s[t])
+                - jnp.maximum(meridional[t], 0.0) * (s[t] - below)
+                - jnp.minimum(meridional[t], 0.0) * (above - s[t])
+            )
+
+
 def dispatch_kernel(
     ny,
     nx,
@@ -50,6 +85,7 @@
     slot,
     convect,
     state_hbm,
+    winds_hbm,
     slots,
     lat_even,
     lat_odd,
@@ -57,15 +93,21 @@
     lon_odd,
     target,
     filled,
+    flow_hbm,
     state,
+    winds,
+    flow,
     chosen,
     choice,
     total,
     edges,
     arrived,
+    left_over,
 ):
-    load = pltpu.make_async_copy(state_hbm, state, arrived)
+    load = pltpu.make_async_copy(state_hbm, state, arrived.at[0])
     load.start()
+    load_winds = pltpu.make_async_copy(winds_hbm, winds, arrived.at[1])
+    load_winds.start()
     width = state.shape[0] // (ny * 2)
     lanes = nx // 2
     lower = choice.shape[1]
@@ -115,11 +157,24 @@
         else:
             total[...] += product
 
+    levels = winds.shape[0] // (4 * ny)
+    share = levels // steps
+    sends = []
     build(0, 0)
     for g in range(steps):
         if g < steps - 1:
             build(g + 1, (g + 1) % 2)
         multiply(g, g % 2)
+        if g == 0:
+            load_winds.wait()
+        for k in range(g * share, (g + 1) * share):
+            advect_level(ny, nx, state, winds, flow, k)
+        for f in range(width // levels):
+            rows = pl.ds((f * levels + g * share) * 2 * ny, share * 2 * ny)
+            sends.append(
+                pltpu.make_async_copy(flow.at[rows, :], flow_hbm.at[rows, :], left_over.at[g, f])
+            )
+            sends[-1].start()
     for h in range(uppers):
         slots[pl.ds(h * lower, lower), :] = total[:, pl.ds(h * width, width)].astype(slots.dtype)
 
@@ -134,13 +189,16 @@
     west, east = edges[pl.ds(0, ny), :], edges[pl.ds(ny, ny), :]
     lon_even[...] = jnp.where(odd, west, east).astype(lon_even.dtype)
     lon_odd[...] = jnp.where(odd, east, west).astype(lon_odd.dtype)
-
-
-def dispatch(dest, slot, convect, state, group):
+    for send in sends:
+        send.wait()
+
+
+def dispatch(dest, slot, convect, state, winds, group):
     ny, nx = dest.shape
     width, count = state.shape[0] // (ny * 2), ny * nx
     uppers, depth = 4, 4 * nx
     lower = count // uppers
+    hbm = pl.BlockSpec(memory_space=pl.ANY)
     vmem = pl.BlockSpec(memory_space=pltpu.VMEM)
     kernel = lambda *refs: dispatch_kernel(ny, nx, *refs)
     shape = jax.ShapeDtypeStruct
@@ -154,16 +212,20 @@
             shape((ny, width), jnp.bfloat16),
             shape((2, ny, nx // 2), jnp.int32),
             shape((group, width), jnp.int32),
+            shape(state.shape, jnp.float32),
         ),
-        in_specs=[vmem, vmem, vmem, pl.BlockSpec(memory_space=pl.ANY)],
-        out_specs=(vmem,) * 7,
+        in_specs=[vmem, vmem, vmem, hbm, hbm],
+        out_specs=(vmem,) * 7 + (hbm,),
         scratch_shapes=[
+            pltpu.VMEM(state.shape, jnp.float32),
+            pltpu.VMEM(winds.shape, jnp.float32),
             pltpu.VMEM(state.shape, jnp.float32),
             pltpu.VMEM((2, depth, uppers * width), jnp.bfloat16),
             pltpu.VMEM((2, lower, depth), jnp.bfloat16),
             pltpu.VMEM((lower, uppers * width), jnp.float32),
             pltpu.VMEM((2 * ny, width), jnp.float32),
-            pltpu.SemaphoreType.DMA,
+            pltpu.SemaphoreType.DMA((2,)),
+            pltpu.SemaphoreType.DMA((4, 2)),
         ],
         compiler_params=pltpu.CompilerParams(vmem_limit_bytes=63 * MIB),
         cost_estimate=pl.CostEstimate(
@@ -172,7 +234,7 @@
             transcendentals=0,
         ),
         name="dispatch",
-    )(dest, slot, convect, state)
+    )(dest, slot, convect, state, winds)
 
 
 def silu_of_half(half):
@@ -269,7 +331,7 @@
     nx,
     target,
     tend_hbm,
-    state_hbm,
+    flow_hbm,
     winds_hbm,
     lat_even,
     lat_odd,
@@ -277,54 +339,44 @@
     lon_odd,
     out_hbm,
     tend,
-    state,
+    flow,
     winds,
     table,
-    low,
-    high,
-    moved,
-    flow,
     arrived,
     left_over,
 ):
-    width = state.shape[0] // (ny * 2)
+    width = flow.shape[0] // (ny * 2)
     lanes = nx // 2
-    subs = ny // SUB
     levels = winds.shape[0] // (4 * ny)
+    fields = width // levels
     count = ny * nx
     copies = [
         pltpu.make_async_copy(tend_hbm, tend, arrived.at[0]),
-        pltpu.make_async_copy(state_hbm, state, arrived.at[1]),
+        pltpu.make_async_copy(flow_hbm, flow, arrived.at[1]),
         pltpu.make_async_copy(winds_hbm, winds, arrived.at[2]),
     ]
     for copy in copies:
         copy.start()
     odd = lax.axis_index("span") == 1
     evens, odds = lon_even[...].astype(jnp.float32), lon_odd[...].astype(jnp.float32)
-    west = jnp.where(odd, evens, odds)
-    east = jnp.where(odd, odds, evens)
+    beside = (jnp.where(odd, evens, odds).T, jnp.where(odd, odds, evens).T)
     odd = lax.axis_index("lat") % 2 == 1
-    for half in range(2):
-        part = pl.ds(half * lanes, lanes)
-        evens, odds = lat_even[:, part].astype(jnp.float32), lat_odd[:, part].astype(jnp.float32)
-        low[half] = jnp.where(odd, evens, odds)
-        high[half] = jnp.where(odd, odds, evens)
+    evens, odds = lat_even[...].astype(jnp.float32), lat_odd[...].astype(jnp.float32)
+    south, north = jnp.where(odd, evens, odds), jnp.where(odd, odds, evens)
     lower = table.shape[1]
     uppers = table.shape[0] // width
     shift, mask = log2(lower), lower - 1
+    lane = lax.broadcasted_iota(jnp.int32, (width, lanes), 1)
     copies[0].wait()
     for h in range(uppers):
         rows = tend[pl.ds(h * lower, lower), :].astype(jnp.float32)
         table[pl.ds(h * width, width), :] = rows.T.astype(table.dtype)
 
-    lane = lax.broadcasted_iota(jnp.int32, (SUB, lanes), 1)
-    line = lax.broadcasted_iota(jnp.int32, (SUB, lanes), 0)
-    tiles = [(sub, half) for sub in range(subs) for half in range(2)]
-
-    def block(r, sub, half):
-        return pl.ds(r * (2 * ny) + (sub * 2 + half) * SUB, SUB)
-
-    def move(y):
+    def wind(component, y, half):
+        first = component * levels * 2 * ny + tile_row(y, half)
+        return jnp.concatenate([winds[pl.ds(first, levels, stride=2 * ny), :]] * fields, axis=0)
+
+    for y in range(ny):
         index = jnp.concatenate([target[half, pl.ds(y, 1), :] for half in range(2)], axis=1)
         wanted = jnp.where(index == count, -1, index & mask)
         candidates = jnp.dot(
@@ -335,62 +387,34 @@
         for h in range(1, uppers):
             change = jnp.where((upper == h)[None], candidates[h], change)
         change = change.reshape(width, nx)
-        for half in range(2):
-            place = pl.ds(tile_row(y, half), width, stride=2 * ny)
-            moved[place, :] = change[:, half * lanes : (half + 1) * lanes]
-
-    def advect(k):
-        zonal = {t: winds[block(k, *t), :] for t in tiles}
-        meridional = {t: winds[block(levels + k, *t), :] for t in tiles}
-        for f in range(width // levels):
-            r = f * levels + k
-            s = {t: state[block(r, *t), :] for t in tiles}
-            first = pltpu.roll(west, (width - r) % width, axis=1)
-            last = pltpu.roll(east, width - 1 - r, axis=1)
-            up = {t: pltpu.roll(s[t], 1, axis=1) for t in tiles}
-            down = {t: pltpu.roll(s[t], lanes - 1, axis=1) for t in tiles}
-            rise = {t: pltpu.roll(s[t], 1, axis=0) for t in tiles}
-            fall = {t: pltpu.roll(s[t], SUB - 1, axis=0) for t in tiles}
-            for sub, half in tiles:
-                t = (sub, half)
-                edge = slice(sub * SUB, (sub + 1) * SUB)
-                left = jnp.where(lane == 0, up[sub, 0] if half else first[edge], up[t])
-                right = jnp.where(lane == lanes - 1, last[edge] if half else down[sub, 1], down[t])
-                under = rise[sub - 1, half] if sub else low[half, pl.ds(r, 1), :]
-                over = fall[sub + 1, half] if sub < subs - 1 else high[half, pl.ds(r, 1), :]
-                below = jnp.where(line == 0, under, rise[t])
-                above = jnp.where(line == SUB - 1, over, fall[t])
-                flow[block(r, *t), :] = (
-                    s[t]
-                    - jnp.maximum(zonal[t], 0.0) * (s[t] - left)
-                    - jnp.minimum(zonal[t], 0.0) * (right - s[t])
-                    - jnp.maximum(meridional[t], 0.0) * (s[t] - below)
-                    - jnp.minimum(meridional[t], 0.0) * (above - s[t])
-                )
-
-    ahead = 2
-    share = levels // (ny - ahead) + 1
-    for y in range(ny):
-        move(y)
-        if y == ahead - 1:
+        if y == 0:
             copies[1].wait()
             copies[2].wait()
-        start = (y - ahead) * share
-        for k in range(max(start, 0), max(min(start + share, levels), 0)):
-            advect(k)
+        for half in range(2):
+            part = slice(half * lanes, (half + 1) * lanes)
+            place = pl.ds(tile_row(y, half), width, stride=2 * ny)
+            zonal = wind(0, y, half)
+            inflow = -jnp.minimum(zonal, 0.0) if half else jnp.maximum(zonal, 0.0)
+            edge = jnp.broadcast_to(beside[half][:, y : y + 1], (width, lanes))
+            there = lane == (lanes - 1 if half else 0)
+            result = flow[place, :] + jnp.where(there, inflow * edge, 0.0)
+            if y == 0:
+                result = result + jnp.maximum(wind(1, y, half), 0.0) * south[:, part]
+            if y == ny - 1:
+                result = result - jnp.minimum(wind(1, y, half), 0.0) * north[:, part]
+            flow[place, :] = result + change[:, part]
     pieces = left_over.shape[0]
-    size = state.shape[0] // pieces
+    size = flow.shape[0] // pieces
     sends = []
     for p in range(pieces):
         rows = pl.ds(p * size, size)
-        flow[rows, :] = flow[rows, :] + moved[rows, :]
         sends.append(pltpu.make_async_copy(flow.at[rows, :], out_hbm.at[rows, :], left_over.at[p]))
         sends[-1].start()
     for send in sends:
         send.wait()
 
 
-def finish(target, tend, state, winds, *edges):
+def finish(target, tend, flow, winds, *edges):
     _, ny, lanes = target.shape
     nx = 2 * lanes
     count, width = tend.shape
@@ -400,18 +424,14 @@
     kernel = lambda *refs: finish_kernel(ny, nx, *refs)
     return pl.pallas_call(
         kernel,
-        out_shape=jax.ShapeDtypeStruct(state.shape, jnp.float32),
+        out_shape=jax.ShapeDtypeStruct(flow.shape, jnp.float32),
         in_specs=[vmem, hbm, hbm, hbm, vmem, vmem, vmem, vmem],
         out_specs=hbm,
         scratch_shapes=[
             pltpu.VMEM(tend.shape, tend.dtype),
-            pltpu.VMEM(state.shape, jnp.float32),
+            pltpu.VMEM(flow.shape, jnp.float32),
             pltpu.VMEM(winds.shape, jnp.float32),
             pltpu.VMEM((uppers * width, count // uppers), jnp.bfloat16),
-            pltpu.VMEM((2, width, lanes), jnp.float32),
-            pltpu.VMEM((2, width, lanes), jnp.float32),
-            pltpu.VMEM(state.shape, jnp.float32),
-            pltpu.VMEM(state.shape, jnp.float32),
             pltpu.SemaphoreType.DMA((3,)),
             pltpu.SemaphoreType.DMA((4,)),
         ],
@@ -422,7 +442,7 @@
             transcendentals=0,
         ),
         name="finish",
-    )(target, tend, state, winds, *edges)
+    )(target, tend, flow, winds, *edges)
 
 
 def to_tiles(field):
@@ -442,8 +462,8 @@
 
     recalled = exchange(memory)
     flat_state, flat_winds = to_tiles(state), to_tiles(winds)
-    columns, lat_even, lat_odd, lon_even, lon_odd, target, filled = dispatch(
-        dest, slot, convect, flat_state, group
+    columns, lat_even, lat_odd, lon_even, lon_odd, target, filled, flow = dispatch(
+        dest, slot, convect, flat_state, flat_winds, group
     )
     loop = ("lon", "span")
     lon_even = swapped(lon_even, loop, 0, True)
@@ -454,7 +474,7 @@
     edges = (lat_even, lat_odd, lon_even)
     renewed, edges = lax.optimization_barrier((renewed, edges))
     new_memory = exchange(renewed)
-    new_state = finish(target, tend, flat_state, flat_winds, *edges, lon_odd)
+    new_state = finish(target, tend, flow, flat_winds, *edges, lon_odd)
     return from_tiles(new_state, state.shape), new_memory
 
 

time: 59.6 us -> 61.4 us (1.030)
  Pallas kernels: 29.7 us -> 31.8 us
  waiting for transfers between devices: 3.55 us -> 2.55 us
  starting transfers between devices: 23.6 us -> 24.3 us
    pallas_call x1, Pallas kernels: 9.16 us -> 10.2 us  [dispatch(): pl.pallas_call(kernel, out_shape=(shape((count, width), jnp.bfloat16), sh...]
    all_to_all x2, waiting for transfers between devices: 2.21 us -> 1.21 us  [exchange(): lax.all_to_all(rows, GROUP_AXES, split_axis=0, concat_axis=0, tiled=True)]
    pallas_call x1, Pallas kernels: 10.7 us -> 11.7 us  [finish(): pl.pallas_call(kernel, out_shape=jax.ShapeDtypeStruct(flow.shape, jnp.flo...]
    all_to_all x2, starting transfers between devices: 13 us -> 13.7 us  [exchange(): lax.all_to_all(rows, GROUP_AXES, split_axis=0, concat_axis=0, tiled=True)]
  transfers between devices with their start and end apart: 6 -> 6, of which waited for: 2 -> 2; matrix products, arithmetic and copies ran while one was open for 0% -> 0% of each run, Pallas kernels for 50% -> 52%
where the time goes in v4:
time: 61.4 us; the launch traced here: 60.9 us
  Pallas kernels  31.8 us (52%)
  starting transfers between devices  24.3 us (40%)
  waiting for transfers between devices  2.55 us (4%)
  local copies, waits for them, and re-layouts  1.57 us (3%)
  between operations  0.74 us (1%)
    all_to_all x2, starting transfers between devices, exchange(): lax.all_to_all(rows, GROUP_AXES, split_axis=0, concat_axis=0, tiled=True)  13.7 us
    pallas_call x1, Pallas kernels, finish(): pl.pallas_call(kernel, out_shape=jax.ShapeDtypeStruct(flow.shape, jnp.flo...  11.7 us
    ppermute x4, starting transfers between devices, swapped(): return lax.ppermute(edge, axis, pairs + [(j, i) for i, j in pairs])  10.7 us
    pallas_call x1, Pallas kernels, dispatch(): pl.pallas_call(kernel, out_shape=(shape((count, width), jnp.bfloat16), sh...  10.2 us
    pallas_call x1, Pallas kernels, network(): pl.pallas_call(kernel, grid=(count // ROWS_MLP,), out_shape=(jax.ShapeDty...  9.9 us
    unnamed x11, local copies, waits for them, and re-layouts  1.57 us
    ppermute x4, waiting for transfers between devices, swapped(): return lax.ppermute(edge, axis, pairs + [(j, i) for i, j in pairs])  1.34 us
  transfers between devices with their start and end apart: 6, of which 2 were waited for; matrix products, arithmetic and copies ran while one was open for 0% of the time, Pallas kernels for 52%

profile of v4, /device:TPU:2, one launch (start us, length us, event | category | flops | bytes accessed | tf_op | source)
XLA Modules:
  0.0 60.9 jit_solution(14290670194874814715)
XLA Ops:
  0.6 7.7 %all-to-all-start = ((bf16[32,128,128]{2,1,0:T(8,128)(2,1)}), bf16[32,128,128]{2,1,0:T(8,128)(2,1)}, u32[]{:S(2)}, u32[]{:S(2)}) async-start(bf16[32,128,128]{2,1,0:T(8,128)(2,1)} %bitcast.20), calls=%async_computation | async-start | bytes 2097152 | tf_op jit(solution)/shard_map/all_to_all | solution.py:23
  8.3 10.2 %dispatch.1 = (bf16[4096,128]{1,0:T(8,128)(2,1)}, bf16[128,256]{1,0:T(8,128)(2,1)}, bf16[128,256]{1,0:T(8,128)(2,1)}, bf16[16,128]{1,0:T(8,128)(2,1)}, bf16[16,1...) custom-call(s32[16,256]{1,0:T(8,128)} %refs_0_.1, s32[16,256]{1,0:T(8,128)} %refs_1_.1, ...), custom_call_target="tpu_custom_call" | custom-call | flops 4294967296 | bytes 3145728 | tf_op jit(solution)/shard_map/dispatch/pallas_call | solution.py:205
  18.5 0.2 collective-permute-start.2
  18.7 0.4 collective-permute-start
  19.1 4.2 %collective-permute-start.1 = (bf16[128,256]{1,0:T(8,128)(2,1)}, bf16[128,256]{1,0:T(8,128)(2,1)S(1)}, u32[]{:S(2)}, u32[]{:S(2)}) collective-permute-start(bf16[128,256]{1,0:T(8,128)(2,1)} %get-tuple-element.23), channel_id=1, source_target_pairs={{2,4},{6,8},{10,12},{14,16},{18,20},{22,24},{26,28},{4,2},{8,6},{1... | collective-permute-start | bytes 196616 | tf_op jit(solution)/shard_map/ppermute | solution.py:19
  23.3 1.2 %all-to-all-done = bf16[32,128,128]{2,1,0:T(8,128)(2,1)} async-done(((bf16[32,128,128]{2,1,0:T(8,128)(2,1)}), bf16[32,128,128]{2,1,0:T(8,128)(2,1)}, u32[]{:S(2)}, u32[]{:S(2)}) %all-to-all-start) | async-done | bytes 1048608 | tf_op jit(solution)/shard_map/all_to_all | solution.py:23
  24.5 9.9 %network.1 = (bf16[4096,128]{1,0:T(8,128)(2,1)}, bf16[4096,128]{1,0:T(8,128)(2,1)}) custom-call(s32[32,128]{1,0:T(8,128)} %get-tuple-element.17.refs_0_, bf16[4096,128]{1,0:T(8,128)(2,1)} %get-tuple-element.18.refs_1_, bf16[4096,128]{1,0:T(8,128)(2,1)} %bitcast.7.refs_2_, bf16[256,512]{1,0:T(8,128)(2,1)} %refs_3_.1, bf16[512,512]{1,0:T(8,128)(2,1)} %refs_4_.1, ...), custom_call_target="tpu_custom_call" | custom-call | flops 6442450944 | bytes 5767168 | tf_op jit(solution)/shard_map/network/pallas_call | solution.py:309
  34.4 0.0 collective-permute-done.2.refs_6_
  34.4 0.0 copy-start.2
  34.4 0.0 collective-permute-done.refs_4_
  34.4 0.0 copy-start
  34.4 0.0 collective-permute-done.1.refs_5_
  34.4 0.0 copy-start.1
  34.5 6.0 %all-to-all-start.1 = ((bf16[32,128,128]{2,1,0:T(8,128)(2,1)}), bf16[32,128,128]{2,1,0:T(8,128)(2,1)S(1)}, u32[]{:S(2)}, u32[]{:S(2)}) async-start(bf16[32,128,128]{2,1,0:T(8,128)(2,1)} %bitcast.21), calls=%async_computation.1 | async-start | bytes 2097152 | tf_op jit(solution)/shard_map/all_to_all | solution.py:23
  40.4 0.0 copy-done.3
  40.4 5.9 %collective-permute-start.3 = (bf16[16,128]{1,0:T(8,128)(2,1)S(1)}, bf16[16,128]{1,0:T(8,128)(2,1)S(1)}, u32[]{:S(2)}, u32[]{:S(2)}) collective-permute-start(bf16[16,128]{1,0:T(8,128)(2,1)S(1)} %copy-done.3), channel_id=1, source_target_pairs={{1,32},{33,64},{65,96},{97,128},{129,160},{161,192},{193,224},{225... | collective-permute-start | bytes 12296 | tf_op jit(solution)/shard_map/ppermute | solution.py:19
  46.3 1.3 %collective-permute-done.3.refs_7_ = bf16[16,128]{1,0:T(8,128)(2,1)S(1)} collective-permute-done((bf16[16,128]{1,0:T(8,128)(2,1)S(1)}, bf16[16,128]{1,0:T(8,128)(2,1)S(1)}, u32[]{:S(2)}, u32[]{:S(2)}) %collective-permute-start.3) | collective-permute-done | bytes 4128 | tf_op jit(solution)/shard_map/ppermute | solution.py:19
  47.7 0.0 copy-done.2
  47.7 0.0 copy-done
  47.7 0.0 copy-done.1
  47.7 0.6 copy-done.4
  48.3 11.7 %finish.1 = f32[4096,128]{1,0:T(8,128)} custom-call(s32[2,16,128]{2,1,0:T(8,128)} %get-tuple-element.16.refs_0_, bf16[4096,128]{1,0:T(8,128)(2,1)} %get-tuple-element.19.refs_1_, f32[4096,128]{1,0:T(8,128)} %get-tuple-element.20.refs_2_, f32[4096,128]{1,0:T(8,128)} %bitcast.24, bf16[128,256]{1,0:T(8,128)(2,1)} %copy-done, bf16[128,256]{1,0:T(8,128)(2,1)} %copy-done.1, ...), custom_call_target="tpu_custom_call" | custom-call | flops 4294967296 | bytes 7340032 | tf_op jit(solution)/shard_map/finish/pallas_call | solution.py:425
  59.9 0.0 all-to-all-done.1
  59.9 1.0 %copy.13 = bf16[4096,128]{1,0:T(8,128)(2,1)} copy(bf16[4096,128]{1,0:T(8,128)(2,1)S(1)} %bitcast.19) | data formatting | bytes 2097152
  (2 shorter events, 0.0 us)
Async XLA Ops:
  0.6 23.9 %all-to-all-start = ((bf16[32,128,128]{2,1,0:T(8,128)(2,1)}), bf16[32,128,128]{2,1,0:T(8,128)(2,1)}, u32[]{:S(2)}, u32[]{:S(2)}) async-start(bf16[32,128,128]{2,1,0:T(8,128)(2,1)} %bitcast.20), calls=%async_computation | async-start | bytes 2097152 | tf_op jit(solution)/shard_map/all_to_all | solution.py:23
  18.5 15.9 %collective-permute-start.2 = (bf16[16,128]{1,0:T(8,128)(2,1)}, bf16[16,128]{1,0:T(8,128)(2,1)S(1)}, u32[]{:S(2)}, u32[]{:S(2)}) collective-permute-start(bf16[16,128]{1,0:T(8,128)(2,1)} %get-tuple-element.24), channel_id=1, source_target_pairs={{0,1},{32,33},{64,65},{96,97},{128,129},{160,161},{192,193},{224,2... | collective-permute-start | bytes 12296 | tf_op jit(solution)/shard_map/ppermute | solution.py:19
  18.7 15.7 %collective-permute-start = (bf16[128,256]{1,0:T(8,128)(2,1)}, bf16[128,256]{1,0:T(8,128)(2,1)S(1)}, u32[]{:S(2)}, u32[]{:S(2)}) collective-permute-start(bf16[128,256]{1,0:T(8,128)(2,1)} %get-tuple-element.22), channel_id=1, source_target_pairs={{0,2},{4,6},{8,10},{12,14},{16,18},{20,22},{24,26},{28,30},{2,0},{... | collective-permute-start | bytes 196616 | tf_op jit(solution)/shard_map/ppermute | solution.py:19
  19.1 15.3 %collective-permute-start.1 = (bf16[128,256]{1,0:T(8,128)(2,1)}, bf16[128,256]{1,0:T(8,128)(2,1)S(1)}, u32[]{:S(2)}, u32[]{:S(2)}) collective-permute-start(bf16[128,256]{1,0:T(8,128)(2,1)} %get-tuple-element.23), channel_id=1, source_target_pairs={{2,4},{6,8},{10,12},{14,16},{18,20},{22,24},{26,28},{4,2},{8,6},{1... | collective-permute-start | bytes 196616 | tf_op jit(solution)/shard_map/ppermute | solution.py:19
  34.4 6.0 %copy-start.3 = (bf16[16,128]{1,0:T(8,128)(2,1)S(1)}, bf16[16,128]{1,0:T(8,128)(2,1)}, u32[]{:S(2)}) copy-start(bf16[16,128]{1,0:T(8,128)(2,1)} %get-tuple-element.28) | copy-start | bytes 12292
  34.4 13.3 %copy-start.2 = (bf16[16,128]{1,0:T(8,128)(2,1)}, bf16[16,128]{1,0:T(8,128)(2,1)S(1)}, u32[]{:S(2)}) copy-start(bf16[16,128]{1,0:T(8,128)(2,1)S(1)} %collective-permute-done.2.refs_6_) | copy-start | bytes 12292
  34.4 13.2 %copy-start = (bf16[128,256]{1,0:T(8,128)(2,1)}, bf16[128,256]{1,0:T(8,128)(2,1)S(1)}, u32[]{:S(2)}) copy-start(bf16[128,256]{1,0:T(8,128)(2,1)S(1)} %collective-permute-done.refs_4_) | copy-start | bytes 196612
  34.4 13.2 %copy-start.1 = (bf16[128,256]{1,0:T(8,128)(2,1)}, bf16[128,256]{1,0:T(8,128)(2,1)S(1)}, u32[]{:S(2)}) copy-start(bf16[128,256]{1,0:T(8,128)(2,1)S(1)} %collective-permute-done.1.refs_5_) | copy-start | bytes 196612
  34.5 25.5 %all-to-all-start.1 = ((bf16[32,128,128]{2,1,0:T(8,128)(2,1)}), bf16[32,128,128]{2,1,0:T(8,128)(2,1)S(1)}, u32[]{:S(2)}, u32[]{:S(2)}) async-start(bf16[32,128,128]{2,1,0:T(8,128)(2,1)} %bitcast.21), calls=%async_computation.1 | async-start | bytes 2097152 | tf_op jit(solution)/shard_map/all_to_all | solution.py:23
  40.4 7.2 %collective-permute-start.3 = (bf16[16,128]{1,0:T(8,128)(2,1)S(1)}, bf16[16,128]{1,0:T(8,128)(2,1)S(1)}, u32[]{:S(2)}, u32[]{:S(2)}) collective-permute-start(bf16[16,128]{1,0:T(8,128)(2,1)S(1)} %copy-done.3), channel_id=1, source_target_pairs={{1,32},{33,64},{65,96},{97,128},{129,160},{161,192},{193,224},{225... | collective-permute-start | bytes 12296 | tf_op jit(solution)/shard_map/ppermute | solution.py:19
  47.7 0.6 copy-start.4

commit v5 on v3

--- a/solution.py
+++ b/solution.py
@@ -292,6 +292,7 @@
     subs = ny // SUB
     levels = winds.shape[0] // (4 * ny)
     count = ny * nx
+    pitch = moved.shape[0] // width
     copies = [
         pltpu.make_async_copy(tend_hbm, tend, arrived.at[0]),
         pltpu.make_async_copy(state_hbm, state, arrived.at[1]),
@@ -336,7 +337,7 @@
             change = jnp.where((upper == h)[None], candidates[h], change)
         change = change.reshape(width, nx)
         for half in range(2):
-            place = pl.ds(tile_row(y, half), width, stride=2 * ny)
+            place = pl.ds(tile_row(y, half), width, stride=pitch)
             moved[place, :] = change[:, half * lanes : (half + 1) * lanes]
 
     def advect(k):
@@ -383,7 +384,9 @@
     sends = []
     for p in range(pieces):
         rows = pl.ds(p * size, size)
-        flow[rows, :] = flow[rows, :] + moved[rows, :]
+        for r in range(p * width // pieces, (p + 1) * width // pieces):
+            here = pl.ds(r * 2 * ny, 2 * ny)
+            flow[here, :] = flow[here, :] + moved[pl.ds(r * pitch, 2 * ny), :]
         sends.append(pltpu.make_async_copy(flow.at[rows, :], out_hbm.at[rows, :], left_over.at[p]))
         sends[-1].start()
     for send in sends:
@@ -410,12 +413,12 @@
             pltpu.VMEM((uppers * width, count // uppers), jnp.bfloat16),
             pltpu.VMEM((2, width, lanes), jnp.float32),
             pltpu.VMEM((2, width, lanes), jnp.float32),
-            pltpu.VMEM(state.shape, jnp.float32),
+            pltpu.VMEM((width * (2 * ny + SUB), lanes), jnp.float32),
             pltpu.VMEM(state.shape, jnp.float32),
             pltpu.SemaphoreType.DMA((3,)),
             pltpu.SemaphoreType.DMA((4,)),
         ],
-        compiler_params=pltpu.CompilerParams(vmem_limit_bytes=VMEM_LIMIT),
+        compiler_params=pltpu.CompilerParams(vmem_limit_bytes=56 * MIB),
         cost_estimate=pl.CostEstimate(
             flops=2 * count * count * width,
             bytes_accessed=14 * count * width,

time: 59.6 us -> 59.3 us (level); the launches traced: 59.2 us -> 58.2 us
  Pallas kernels: 29.7 us -> 28.7 us
    pallas_call x1, Pallas kernels: 10.7 us -> 9.71 us  [finish(): pl.pallas_call(kernel, out_shape=jax.ShapeDtypeStruct(state.shape, jnp.fl...]
  transfers between devices with their start and end apart: 6 -> 6, of which waited for: 2 -> 2; matrix products, arithmetic and copies ran while one was open for 0% -> 0% of each run, Pallas kernels for 50% -> 49%
where the time goes in v5:
time: 59.3 us; the launch traced here: 58.2 us
  Pallas kernels  28.7 us (48%)
  starting transfers between devices  23.6 us (40%)
  waiting for transfers between devices  3.55 us (6%)
  local copies, waits for them, and re-layouts  1.55 us (3%)
  between operations  0.74 us (1%)
    all_to_all x2, starting transfers between devices, exchange(): lax.all_to_all(rows, GROUP_AXES, split_axis=0, concat_axis=0, tiled=True)  13 us
    ppermute x4, starting transfers between devices, swapped(): return lax.ppermute(edge, axis, pairs + [(j, i) for i, j in pairs])  10.7 us
    pallas_call x1, Pallas kernels, network(): pl.pallas_call(kernel, grid=(count // ROWS_MLP,), out_shape=(jax.ShapeDty...  9.88 us
    pallas_call x1, Pallas kernels, finish(): pl.pallas_call(kernel, out_shape=jax.ShapeDtypeStruct(state.shape, jnp.fl...  9.71 us
    pallas_call x1, Pallas kernels, dispatch(): pl.pallas_call(kernel, out_shape=(shape((count, width), jnp.bfloat16), sh...  9.16 us
    all_to_all x2, waiting for transfers between devices, exchange(): lax.all_to_all(rows, GROUP_AXES, split_axis=0, concat_axis=0, tiled=True)  2.21 us
    unnamed x11, local copies, waits for them, and re-layouts  1.55 us
    ppermute x4, waiting for transfers between devices, swapped(): return lax.ppermute(edge, axis, pairs + [(j, i) for i, j in pairs])  1.34 us
  transfers between devices with their start and end apart: 6, of which 2 were waited for; matrix products, arithmetic and copies ran while one was open for 0% of the time, Pallas kernels for 49%

profile of v5, /device:TPU:2, one launch (start us, length us, event | category | flops | bytes accessed | tf_op | source)
XLA Modules:
  0.0 58.2 jit_solution(5286994473894661423)
XLA Ops:
  0.6 7.7 %all-to-all-start = ((bf16[32,128,128]{2,1,0:T(8,128)(2,1)}), bf16[32,128,128]{2,1,0:T(8,128)(2,1)}, u32[]{:S(2)}, u32[]{:S(2)}) async-start(bf16[32,128,128]{2,1,0:T(8,128)(2,1)} %bitcast.20), calls=%async_computation | async-start | bytes 2097152 | tf_op jit(solution)/shard_map/all_to_all | solution.py:23
  8.3 9.2 %dispatch.1 = (bf16[4096,128]{1,0:T(8,128)(2,1)}, bf16[128,256]{1,0:T(8,128)(2,1)}, bf16[128,256]{1,0:T(8,128)(2,1)}, bf16[16,128]{1,0:T(8,128)(2,1)}, bf16[16,1...) custom-call(s32[16,256]{1,0:T(8,128)} %refs_0_.1, s32[16,256]{1,0:T(8,128)} %refs_1_.1, ...), custom_call_target="tpu_custom_call" | custom-call | flops 4294967296 | bytes 3145728 | tf_op jit(solution)/shard_map/dispatch/pallas_call | solution.py:147
  17.5 0.2 collective-permute-start.2
  17.7 0.4 collective-permute-start
  18.1 4.2 %collective-permute-start.1 = (bf16[128,256]{1,0:T(8,128)(2,1)}, bf16[128,256]{1,0:T(8,128)(2,1)S(1)}, u32[]{:S(2)}, u32[]{:S(2)}) collective-permute-start(bf16[128,256]{1,0:T(8,128)(2,1)} %get-tuple-element.21), channel_id=1, source_target_pairs={{2,4},{6,8},{10,12},{14,16},{18,20},{22,24},{26,28},{4,2},{8,6},{1... | collective-permute-start | bytes 196616 | tf_op jit(solution)/shard_map/ppermute | solution.py:19
  22.3 2.2 %all-to-all-done = bf16[32,128,128]{2,1,0:T(8,128)(2,1)} async-done(((bf16[32,128,128]{2,1,0:T(8,128)(2,1)}), bf16[32,128,128]{2,1,0:T(8,128)(2,1)}, u32[]{:S(2)}, u32[]{:S(2)}) %all-to-all-start) | async-done | bytes 1048608 | tf_op jit(solution)/shard_map/all_to_all | solution.py:23
  24.5 9.9 %network.1 = (bf16[4096,128]{1,0:T(8,128)(2,1)}, bf16[4096,128]{1,0:T(8,128)(2,1)}) custom-call(s32[32,128]{1,0:T(8,128)} %get-tuple-element.16.refs_0_, bf16[4096,128]{1,0:T(8,128)(2,1)} %get-tuple-element.17.refs_1_, bf16[4096,128]{1,0:T(8,128)(2,1)} %bitcast.4.refs_2_, bf16[256,512]{1,0:T(8,128)(2,1)} %refs_3_.1, bf16[512,512]{1,0:T(8,128)(2,1)} %refs_4_.1, ...), custom_call_target="tpu_custom_call" | custom-call | flops 6442450944 | bytes 5767168 | tf_op jit(solution)/shard_map/network/pallas_call | solution.py:247
  34.4 0.0 collective-permute-done.2.refs_6_
  34.4 0.0 copy-start.2
  34.4 0.0 collective-permute-done.refs_4_
  34.4 0.0 copy-start
  34.4 0.0 collective-permute-done.1.refs_5_
  34.4 0.0 copy-start.1
  34.4 5.3 %all-to-all-start.1 = ((bf16[32,128,128]{2,1,0:T(8,128)(2,1)}), bf16[32,128,128]{2,1,0:T(8,128)(2,1)S(1)}, u32[]{:S(2)}, u32[]{:S(2)}) async-start(bf16[32,128,128]{2,1,0:T(8,128)(2,1)} %bitcast.21), calls=%async_computation.1 | async-start | bytes 2097152 | tf_op jit(solution)/shard_map/all_to_all | solution.py:23
  39.7 0.0 copy-done.3
  39.7 5.9 %collective-permute-start.3 = (bf16[16,128]{1,0:T(8,128)(2,1)S(1)}, bf16[16,128]{1,0:T(8,128)(2,1)S(1)}, u32[]{:S(2)}, u32[]{:S(2)}) collective-permute-start(bf16[16,128]{1,0:T(8,128)(2,1)S(1)} %copy-done.3), channel_id=1, source_target_pairs={{1,32},{33,64},{65,96},{97,128},{129,160},{161,192},{193,224},{225... | collective-permute-start | bytes 12296 | tf_op jit(solution)/shard_map/ppermute | solution.py:19
  45.6 1.3 %collective-permute-done.3.refs_7_ = bf16[16,128]{1,0:T(8,128)(2,1)S(1)} collective-permute-done((bf16[16,128]{1,0:T(8,128)(2,1)S(1)}, bf16[16,128]{1,0:T(8,128)(2,1)S(1)}, u32[]{:S(2)}, u32[]{:S(2)}) %collective-permute-start.3) | collective-permute-done | bytes 4128 | tf_op jit(solution)/shard_map/ppermute | solution.py:19
  46.9 0.0 copy-done.2
  46.9 0.0 copy-done
  46.9 0.0 copy-done.1
  46.9 0.6 copy-done.4
  47.5 9.7 %finish.1 = f32[4096,128]{1,0:T(8,128)} custom-call(s32[2,16,128]{2,1,0:T(8,128)} %get-tuple-element.15.refs_0_, bf16[4096,128]{1,0:T(8,128)(2,1)} %get-tuple-element.18.refs_1_, f32[4096,128]{1,0:T(8,128)} %bitcast.23, f32[4096,128]{1,0:T(8,128)} %bitcast.24, bf16[128,256]{1,0:T(8,128)(2,1)} %copy-done, bf16[128,256]{1,0:T(8,128)(2,1)} %copy-done.1, ...), custom_call_target="tpu_custom_call" | custom-call | flops 4294967296 | bytes 7340032 | tf_op jit(solution)/shard_map/finish/pallas_call | solution.py:404
  57.2 0.0 all-to-all-done.1
  57.2 1.0 %copy.13 = bf16[4096,128]{1,0:T(8,128)(2,1)} copy(bf16[4096,128]{1,0:T(8,128)(2,1)S(1)} %bitcast.19) | data formatting | bytes 2097152
  (2 shorter events, 0.0 us)
Async XLA Ops:
  0.6 23.9 %all-to-all-start = ((bf16[32,128,128]{2,1,0:T(8,128)(2,1)}), bf16[32,128,128]{2,1,0:T(8,128)(2,1)}, u32[]{:S(2)}, u32[]{:S(2)}) async-start(bf16[32,128,128]{2,1,0:T(8,128)(2,1)} %bitcast.20), calls=%async_computation | async-start | bytes 2097152 | tf_op jit(solution)/shard_map/all_to_all | solution.py:23
  17.5 16.9 %collective-permute-start.2 = (bf16[16,128]{1,0:T(8,128)(2,1)}, bf16[16,128]{1,0:T(8,128)(2,1)S(1)}, u32[]{:S(2)}, u32[]{:S(2)}) collective-permute-start(bf16[16,128]{1,0:T(8,128)(2,1)} %get-tuple-element.22), channel_id=1, source_target_pairs={{0,1},{32,33},{64,65},{96,97},{128,129},{160,161},{192,193},{224,2... | collective-permute-start | bytes 12296 | tf_op jit(solution)/shard_map/ppermute | solution.py:19
  17.7 16.7 %collective-permute-start = (bf16[128,256]{1,0:T(8,128)(2,1)}, bf16[128,256]{1,0:T(8,128)(2,1)S(1)}, u32[]{:S(2)}, u32[]{:S(2)}) collective-permute-start(bf16[128,256]{1,0:T(8,128)(2,1)} %get-tuple-element.20), channel_id=1, source_target_pairs={{0,2},{4,6},{8,10},{12,14},{16,18},{20,22},{24,26},{28,30},{2,0},{... | collective-permute-start | bytes 196616 | tf_op jit(solution)/shard_map/ppermute | solution.py:19
  18.1 16.3 %collective-permute-start.1 = (bf16[128,256]{1,0:T(8,128)(2,1)}, bf16[128,256]{1,0:T(8,128)(2,1)S(1)}, u32[]{:S(2)}, u32[]{:S(2)}) collective-permute-start(bf16[128,256]{1,0:T(8,128)(2,1)} %get-tuple-element.21), channel_id=1, source_target_pairs={{2,4},{6,8},{10,12},{14,16},{18,20},{22,24},{26,28},{4,2},{8,6},{1... | collective-permute-start | bytes 196616 | tf_op jit(solution)/shard_map/ppermute | solution.py:19
  34.4 5.3 %copy-start.3 = (bf16[16,128]{1,0:T(8,128)(2,1)S(1)}, bf16[16,128]{1,0:T(8,128)(2,1)}, u32[]{:S(2)}) copy-start(bf16[16,128]{1,0:T(8,128)(2,1)} %get-tuple-element.26) | copy-start | bytes 12292
  34.4 12.5 %copy-start.2 = (bf16[16,128]{1,0:T(8,128)(2,1)}, bf16[16,128]{1,0:T(8,128)(2,1)S(1)}, u32[]{:S(2)}) copy-start(bf16[16,128]{1,0:T(8,128)(2,1)S(1)} %collective-permute-done.2.refs_6_) | copy-start | bytes 12292
  34.4 12.5 %copy-start = (bf16[128,256]{1,0:T(8,128)(2,1)}, bf16[128,256]{1,0:T(8,128)(2,1)S(1)}, u32[]{:S(2)}) copy-start(bf16[128,256]{1,0:T(8,128)(2,1)S(1)} %collective-permute-done.refs_4_) | copy-start | bytes 196612
  34.4 12.5 %copy-start.1 = (bf16[128,256]{1,0:T(8,128)(2,1)}, bf16[128,256]{1,0:T(8,128)(2,1)S(1)}, u32[]{:S(2)}) copy-start(bf16[128,256]{1,0:T(8,128)(2,1)S(1)} %collective-permute-done.1.refs_5_) | copy-start | bytes 196612
  34.4 22.8 %all-to-all-start.1 = ((bf16[32,128,128]{2,1,0:T(8,128)(2,1)}), bf16[32,128,128]{2,1,0:T(8,128)(2,1)S(1)}, u32[]{:S(2)}, u32[]{:S(2)}) async-start(bf16[32,128,128]{2,1,0:T(8,128)(2,1)} %bitcast.21), calls=%async_computation.1 | async-start | bytes 2097152 | tf_op jit(solution)/shard_map/all_to_all | solution.py:23
  39.7 7.2 %collective-permute-start.3 = (bf16[16,128]{1,0:T(8,128)(2,1)S(1)}, bf16[16,128]{1,0:T(8,128)(2,1)S(1)}, u32[]{:S(2)}, u32[]{:S(2)}) collective-permute-start(bf16[16,128]{1,0:T(8,128)(2,1)S(1)} %copy-done.3), channel_id=1, source_target_pairs={{1,32},{33,64},{65,96},{97,128},{129,160},{161,192},{193,224},{225... | collective-permute-start | bytes 12296 | tf_op jit(solution)/shard_map/ppermute | solution.py:19
  46.9 0.6 copy-start.4

commit v6 on v5

--- a/solution.py
+++ b/solution.py
@@ -8,7 +8,7 @@
 GROUP_AXES = ("lat", "span")
 MIB = 1024 * 1024
 ROWS_MLP = 2048
-PART = 1024
+PART = 512
 VMEM_LIMIT = 60 * MIB
 SUB = 8
 

time: 59.3 us -> 59.3 us (level)
  no operation moved by 1% of the time
where the time goes in v6:
time: 59.3 us; the launch traced here: 58.2 us
  Pallas kernels  28.8 us (49%)
  starting transfers between devices  23.6 us (40%)
  waiting for transfers between devices  3.55 us (6%)
  local copies, waits for them, and re-layouts  1.55 us (3%)
  between operations  0.74 us (1%)
    all_to_all x2, starting transfers between devices, exchange(): lax.all_to_all(rows, GROUP_AXES, split_axis=0, concat_axis=0, tiled=True)  13 us
    ppermute x4, starting transfers between devices, swapped(): return lax.ppermute(edge, axis, pairs + [(j, i) for i, j in pairs])  10.7 us
    pallas_call x1, Pallas kernels, network(): pl.pallas_call(kernel, grid=(count // ROWS_MLP,), out_shape=(jax.ShapeDty...  9.91 us
    pallas_call x1, Pallas kernels, finish(): pl.pallas_call(kernel, out_shape=jax.ShapeDtypeStruct(state.shape, jnp.fl...  9.72 us
    pallas_call x1, Pallas kernels, dispatch(): pl.pallas_call(kernel, out_shape=(shape((count, width), jnp.bfloat16), sh...  9.16 us
    all_to_all x2, waiting for transfers between devices, exchange(): lax.all_to_all(rows, GROUP_AXES, split_axis=0, concat_axis=0, tiled=True)  2.21 us
    unnamed x11, local copies, waits for them, and re-layouts  1.55 us
    ppermute x4, waiting for transfers between devices, swapped(): return lax.ppermute(edge, axis, pairs + [(j, i) for i, j in pairs])  1.34 us
  transfers between devices with their start and end apart: 6, of which 2 were waited for; matrix products, arithmetic and copies ran while one was open for 0% of the time, Pallas kernels for 49%

profile of v6, /device:TPU:2, one launch (start us, length us, event | category | flops | bytes accessed | tf_op | source)
XLA Modules:
  0.0 58.2 jit_solution(4505374745930313869)
XLA Ops:
  0.6 7.7 %all-to-all-start = ((bf16[32,128,128]{2,1,0:T(8,128)(2,1)}), bf16[32,128,128]{2,1,0:T(8,128)(2,1)}, u32[]{:S(2)}, u32[]{:S(2)}) async-start(bf16[32,128,128]{2,1,0:T(8,128)(2,1)} %bitcast.20), calls=%async_computation | async-start | bytes 2097152 | tf_op jit(solution)/shard_map/all_to_all | solution.py:23
  8.3 9.2 %dispatch.1 = (bf16[4096,128]{1,0:T(8,128)(2,1)}, bf16[128,256]{1,0:T(8,128)(2,1)}, bf16[128,256]{1,0:T(8,128)(2,1)}, bf16[16,128]{1,0:T(8,128)(2,1)}, bf16[16,1...) custom-call(s32[16,256]{1,0:T(8,128)} %refs_0_.1, s32[16,256]{1,0:T(8,128)} %refs_1_.1, ...), custom_call_target="tpu_custom_call" | custom-call | flops 4294967296 | bytes 3145728 | tf_op jit(solution)/shard_map/dispatch/pallas_call | solution.py:147
  17.5 0.2 collective-permute-start.2
  17.7 0.4 collective-permute-start
  18.1 4.2 %collective-permute-start.1 = (bf16[128,256]{1,0:T(8,128)(2,1)}, bf16[128,256]{1,0:T(8,128)(2,1)S(1)}, u32[]{:S(2)}, u32[]{:S(2)}) collective-permute-start(bf16[128,256]{1,0:T(8,128)(2,1)} %get-tuple-element.21), channel_id=1, source_target_pairs={{2,4},{6,8},{10,12},{14,16},{18,20},{22,24},{26,28},{4,2},{8,6},{1... | collective-permute-start | bytes 196616 | tf_op jit(solution)/shard_map/ppermute | solution.py:19
  22.3 2.2 %all-to-all-done = bf16[32,128,128]{2,1,0:T(8,128)(2,1)} async-done(((bf16[32,128,128]{2,1,0:T(8,128)(2,1)}), bf16[32,128,128]{2,1,0:T(8,128)(2,1)}, u32[]{:S(2)}, u32[]{:S(2)}) %all-to-all-start) | async-done | bytes 1048608 | tf_op jit(solution)/shard_map/all_to_all | solution.py:23
  24.5 9.9 %network.1 = (bf16[4096,128]{1,0:T(8,128)(2,1)}, bf16[4096,128]{1,0:T(8,128)(2,1)}) custom-call(s32[32,128]{1,0:T(8,128)} %get-tuple-element.16.refs_0_, bf16[4096,128]{1,0:T(8,128)(2,1)} %get-tuple-element.17.refs_1_, bf16[4096,128]{1,0:T(8,128)(2,1)} %bitcast.4.refs_2_, bf16[256,512]{1,0:T(8,128)(2,1)} %refs_3_.1, bf16[512,512]{1,0:T(8,128)(2,1)} %refs_4_.1, ...), custom_call_target="tpu_custom_call" | custom-call | flops 6442450944 | bytes 5767168 | tf_op jit(solution)/shard_map/network/pallas_call | solution.py:247
  34.4 0.0 collective-permute-done.2.refs_6_
  34.4 0.0 copy-start.2
  34.4 0.0 collective-permute-done.refs_4_
  34.4 0.0 copy-start
  34.4 0.0 collective-permute-done.1.refs_5_
  34.5 0.0 copy-start.1
  34.5 5.3 %all-to-all-start.1 = ((bf16[32,128,128]{2,1,0:T(8,128)(2,1)}), bf16[32,128,128]{2,1,0:T(8,128)(2,1)S(1)}, u32[]{:S(2)}, u32[]{:S(2)}) async-start(bf16[32,128,128]{2,1,0:T(8,128)(2,1)} %bitcast.21), calls=%async_computation.1 | async-start | bytes 2097152 | tf_op jit(solution)/shard_map/all_to_all | solution.py:23
  39.7 0.0 copy-done.3
  39.7 5.9 %collective-permute-start.3 = (bf16[16,128]{1,0:T(8,128)(2,1)S(1)}, bf16[16,128]{1,0:T(8,128)(2,1)S(1)}, u32[]{:S(2)}, u32[]{:S(2)}) collective-permute-start(bf16[16,128]{1,0:T(8,128)(2,1)S(1)} %copy-done.3), channel_id=1, source_target_pairs={{1,32},{33,64},{65,96},{97,128},{129,160},{161,192},{193,224},{225... | collective-permute-start | bytes 12296 | tf_op jit(solution)/shard_map/ppermute | solution.py:19
  45.6 1.3 %collective-permute-done.3.refs_7_ = bf16[16,128]{1,0:T(8,128)(2,1)S(1)} collective-permute-done((bf16[16,128]{1,0:T(8,128)(2,1)S(1)}, bf16[16,128]{1,0:T(8,128)(2,1)S(1)}, u32[]{:S(2)}, u32[]{:S(2)}) %collective-permute-start.3) | collective-permute-done | bytes 4128 | tf_op jit(solution)/shard_map/ppermute | solution.py:19
  47.0 0.0 copy-done.2
  47.0 0.0 copy-done
  47.0 0.0 copy-done.1
  47.0 0.6 copy-done.4
  47.5 9.7 %finish.1 = f32[4096,128]{1,0:T(8,128)} custom-call(s32[2,16,128]{2,1,0:T(8,128)} %get-tuple-element.15.refs_0_, bf16[4096,128]{1,0:T(8,128)(2,1)} %get-tuple-element.18.refs_1_, f32[4096,128]{1,0:T(8,128)} %bitcast.23, f32[4096,128]{1,0:T(8,128)} %bitcast.24, bf16[128,256]{1,0:T(8,128)(2,1)} %copy-done, bf16[128,256]{1,0:T(8,128)(2,1)} %copy-done.1, ...), custom_call_target="tpu_custom_call" | custom-call | flops 4294967296 | bytes 7340032 | tf_op jit(solution)/shard_map/finish/pallas_call | solution.py:404
  57.2 0.0 all-to-all-done.1
  57.3 1.0 %copy.13 = bf16[4096,128]{1,0:T(8,128)(2,1)} copy(bf16[4096,128]{1,0:T(8,128)(2,1)S(1)} %bitcast.19) | data formatting | bytes 2097152
  (2 shorter events, 0.0 us)
Async XLA Ops:
  0.6 23.9 %all-to-all-start = ((bf16[32,128,128]{2,1,0:T(8,128)(2,1)}), bf16[32,128,128]{2,1,0:T(8,128)(2,1)}, u32[]{:S(2)}, u32[]{:S(2)}) async-start(bf16[32,128,128]{2,1,0:T(8,128)(2,1)} %bitcast.20), calls=%async_computation | async-start | bytes 2097152 | tf_op jit(solution)/shard_map/all_to_all | solution.py:23
  17.5 16.9 %collective-permute-start.2 = (bf16[16,128]{1,0:T(8,128)(2,1)}, bf16[16,128]{1,0:T(8,128)(2,1)S(1)}, u32[]{:S(2)}, u32[]{:S(2)}) collective-permute-start(bf16[16,128]{1,0:T(8,128)(2,1)} %get-tuple-element.22), channel_id=1, source_target_pairs={{0,1},{32,33},{64,65},{96,97},{128,129},{160,161},{192,193},{224,2... | collective-permute-start | bytes 12296 | tf_op jit(solution)/shard_map/ppermute | solution.py:19
  17.7 16.7 %collective-permute-start = (bf16[128,256]{1,0:T(8,128)(2,1)}, bf16[128,256]{1,0:T(8,128)(2,1)S(1)}, u32[]{:S(2)}, u32[]{:S(2)}) collective-permute-start(bf16[128,256]{1,0:T(8,128)(2,1)} %get-tuple-element.20), channel_id=1, source_target_pairs={{0,2},{4,6},{8,10},{12,14},{16,18},{20,22},{24,26},{28,30},{2,0},{... | collective-permute-start | bytes 196616 | tf_op jit(solution)/shard_map/ppermute | solution.py:19
  18.1 16.4 %collective-permute-start.1 = (bf16[128,256]{1,0:T(8,128)(2,1)}, bf16[128,256]{1,0:T(8,128)(2,1)S(1)}, u32[]{:S(2)}, u32[]{:S(2)}) collective-permute-start(bf16[128,256]{1,0:T(8,128)(2,1)} %get-tuple-element.21), channel_id=1, source_target_pairs={{2,4},{6,8},{10,12},{14,16},{18,20},{22,24},{26,28},{4,2},{8,6},{1... | collective-permute-start | bytes 196616 | tf_op jit(solution)/shard_map/ppermute | solution.py:19
  34.4 5.3 %copy-start.3 = (bf16[16,128]{1,0:T(8,128)(2,1)S(1)}, bf16[16,128]{1,0:T(8,128)(2,1)}, u32[]{:S(2)}) copy-start(bf16[16,128]{1,0:T(8,128)(2,1)} %get-tuple-element.26) | copy-start | bytes 12292
  34.4 12.5 %copy-start.2 = (bf16[16,128]{1,0:T(8,128)(2,1)}, bf16[16,128]{1,0:T(8,128)(2,1)S(1)}, u32[]{:S(2)}) copy-start(bf16[16,128]{1,0:T(8,128)(2,1)S(1)} %collective-permute-done.2.refs_6_) | copy-start | bytes 12292
  34.4 12.5 %copy-start = (bf16[128,256]{1,0:T(8,128)(2,1)}, bf16[128,256]{1,0:T(8,128)(2,1)S(1)}, u32[]{:S(2)}) copy-start(bf16[128,256]{1,0:T(8,128)(2,1)S(1)} %collective-permute-done.refs_4_) | copy-start | bytes 196612
  34.5 12.5 %copy-start.1 = (bf16[128,256]{1,0:T(8,128)(2,1)}, bf16[128,256]{1,0:T(8,128)(2,1)S(1)}, u32[]{:S(2)}) copy-start(bf16[128,256]{1,0:T(8,128)(2,1)S(1)} %collective-permute-done.1.refs_5_) | copy-start | bytes 196612
  34.5 22.8 %all-to-all-start.1 = ((bf16[32,128,128]{2,1,0:T(8,128)(2,1)}), bf16[32,128,128]{2,1,0:T(8,128)(2,1)S(1)}, u32[]{:S(2)}, u32[]{:S(2)}) async-start(bf16[32,128,128]{2,1,0:T(8,128)(2,1)} %bitcast.21), calls=%async_computation.1 | async-start | bytes 2097152 | tf_op jit(solution)/shard_map/all_to_all | solution.py:23
  39.7 7.2 %collective-permute-start.3 = (bf16[16,128]{1,0:T(8,128)(2,1)S(1)}, bf16[16,128]{1,0:T(8,128)(2,1)S(1)}, u32[]{:S(2)}, u32[]{:S(2)}) collective-permute-start(bf16[16,128]{1,0:T(8,128)(2,1)S(1)} %copy-done.3), channel_id=1, source_target_pairs={{1,32},{33,64},{65,96},{97,128},{129,160},{161,192},{193,224},{225... | collective-permute-start | bytes 12296 | tf_op jit(solution)/shard_map/ppermute | solution.py:19
  47.0 0.6 copy-start.4

commit v7 on v6

--- a/solution.py
+++ b/solution.py
@@ -50,6 +50,9 @@
     slot,
     convect,
     state_hbm,
+    w_in_hbm,
+    w_mid_hbm,
+    w_deep_hbm,
     slots,
     lat_even,
     lat_odd,
@@ -57,15 +60,28 @@
     lon_odd,
     target,
     filled,
+    half_in,
+    half_mid,
+    half_deep,
     state,
+    w_in,
+    w_mid,
+    w_deep,
     chosen,
     choice,
     total,
     edges,
     arrived,
 ):
-    load = pltpu.make_async_copy(state_hbm, state, arrived)
+    load = pltpu.make_async_copy(state_hbm, state, arrived.at[0])
     load.start()
+    loads = [
+        pltpu.make_async_copy(w_in_hbm, w_in, arrived.at[1]),
+        pltpu.make_async_copy(w_mid_hbm, w_mid, arrived.at[2]),
+        pltpu.make_async_copy(w_deep_hbm, w_deep, arrived.at[3]),
+    ]
+    for weights in loads:
+        weights.start()
     width = state.shape[0] // (ny * 2)
     lanes = nx // 2
     lower = choice.shape[1]
@@ -134,9 +150,13 @@
     west, east = edges[pl.ds(0, ny), :], edges[pl.ds(ny, ny), :]
     lon_even[...] = jnp.where(odd, west, east).astype(lon_even.dtype)
     lon_odd[...] = jnp.where(odd, east, west).astype(lon_odd.dtype)
-
-
-def dispatch(dest, slot, convect, state, group):
+    for weights in loads:
+        weights.wait()
+    for half, weights in ((half_in, w_in), (half_mid, w_mid), (half_deep, w_deep)):
+        half[...] = weights[...] * jnp.bfloat16(0.5)
+
+
+def dispatch(dest, slot, convect, state, weights, group):
     ny, nx = dest.shape
     width, count = state.shape[0] // (ny * 2), ny * nx
     uppers, depth = 4, 4 * nx
@@ -154,16 +174,20 @@
             shape((ny, width), jnp.bfloat16),
             shape((2, ny, nx // 2), jnp.int32),
             shape((group, width), jnp.int32),
-        ),
-        in_specs=[vmem, vmem, vmem, pl.BlockSpec(memory_space=pl.ANY)],
-        out_specs=(vmem,) * 7,
+        )
+        + tuple(shape(w.shape, w.dtype) for w in weights),
+        in_specs=[vmem, vmem, vmem] + [pl.BlockSpec(memory_space=pl.ANY)] * 4,
+        out_specs=(vmem,) * 10,
         scratch_shapes=[
             pltpu.VMEM(state.shape, jnp.float32),
+        ]
+        + [pltpu.VMEM(w.shape, w.dtype) for w in weights]
+        + [
             pltpu.VMEM((2, depth, uppers * width), jnp.bfloat16),
             pltpu.VMEM((2, lower, depth), jnp.bfloat16),
             pltpu.VMEM((lower, uppers * width), jnp.float32),
             pltpu.VMEM((2 * ny, width), jnp.float32),
-            pltpu.SemaphoreType.DMA,
+            pltpu.SemaphoreType.DMA((4,)),
         ],
         compiler_params=pltpu.CompilerParams(vmem_limit_bytes=63 * MIB),
         cost_estimate=pl.CostEstimate(
@@ -172,7 +196,7 @@
             transcendentals=0,
         ),
         name="dispatch",
-    )(dest, slot, convect, state)
+    )(dest, slot, convect, state, *weights)
 
 
 def silu_of_half(half):
@@ -184,23 +208,26 @@
     filled,
     columns,
     recalled,
-    w_in,
-    w_mid,
-    w_deep,
-    w_out,
+    half_in,
+    half_mid_hbm,
+    half_deep_hbm,
+    w_out_hbm,
     tend,
     renewed,
-    half_in,
     half_mid,
     half_deep,
+    w_out,
+    arrived,
 ):
-    @pl.when(pl.program_id(0) == 0)
-    def _():
-        for half, weights in ((half_in, w_in), (half_mid, w_mid), (half_deep, w_deep)):
-            half[...] = weights[...] * jnp.bfloat16(0.5)
-
+    loads = [
+        pltpu.make_async_copy(half_mid_hbm, half_mid, arrived.at[0]),
+        pltpu.make_async_copy(half_deep_hbm, half_deep, arrived.at[1]),
+        pltpu.make_async_copy(w_out_hbm, w_out, arrived.at[2]),
+    ]
+    for load in loads:
+        load.start()
     width = columns.shape[1]
-    size, wide = PART, w_in.shape[1]
+    size, wide = PART, half_in.shape[1]
     parts = columns.shape[0] // size
     rows = [pl.ds(p * size, size) for p in range(parts)]
     values = [[columns[r, :], recalled[r, :]] for r in rows]
@@ -210,7 +237,9 @@
         sums, kept = waiting.pop(0)
         kept.append(silu_of_half(sums).astype(jnp.bfloat16))
 
-    for weights in (half_in, half_mid, half_deep):
+    for i, weights in enumerate((half_in, half_mid, half_deep)):
+        if i > 0:
+            loads[i - 1].wait()
         following = [[] for _ in rows]
         for p in range(parts):
             joined = jnp.concatenate(values[p], axis=1)
@@ -222,6 +251,7 @@
                     settle()
         values = following
     settle()
+    loads[2].wait()
     owners = size // capacity
     place = lax.broadcasted_iota(jnp.int32, (capacity, width), 0)
     for p in range(parts):
@@ -251,9 +281,10 @@
             jax.ShapeDtypeStruct((count, width), jnp.bfloat16),
             jax.ShapeDtypeStruct((count, width), jnp.bfloat16),
         ),
-        in_specs=[counts, rows, rows] + [whole(w) for w in weights],
+        in_specs=[counts, rows, rows, whole(w_in)] + [pl.BlockSpec(memory_space=pl.ANY)] * 3,
         out_specs=(rows, rows),
-        scratch_shapes=[pltpu.VMEM(w.shape, w.dtype) for w in weights[:3]],
+        scratch_shapes=[pltpu.VMEM(w.shape, w.dtype) for w in weights[1:]]
+        + [pltpu.SemaphoreType.DMA((3,))],
         compiler_params=pltpu.CompilerParams(vmem_limit_bytes=VMEM_LIMIT),
         cost_estimate=pl.CostEstimate(
             flops=2 * count * sum(w.size for w in weights),
@@ -445,15 +476,15 @@
 
     recalled = exchange(memory)
     flat_state, flat_winds = to_tiles(state), to_tiles(winds)
-    columns, lat_even, lat_odd, lon_even, lon_odd, target, filled = dispatch(
-        dest, slot, convect, flat_state, group
+    columns, lat_even, lat_odd, lon_even, lon_odd, target, filled, *halves = dispatch(
+        dest, slot, convect, flat_state, (w_in, w_mid, w_deep), group
     )
     loop = ("lon", "span")
     lon_even = swapped(lon_even, loop, 0, True)
     lon_odd = swapped(lon_odd, loop, 1, True)
     lat_even = swapped(lat_even, "lat", 0, False)
     lat_odd = swapped(lat_odd, "lat", 1, False)
-    tend, renewed = network(filled, columns, recalled, w_in, w_mid, w_deep, w_out)
+    tend, renewed = network(filled, columns, recalled, *halves, w_out)
     edges = (lat_even, lat_odd, lon_even)
     renewed, edges = lax.optimization_barrier((renewed, edges))
     new_memory = exchange(renewed)

time: 59.3 us -> 61.7 us (1.040)
  Pallas kernels: 28.8 us -> 31.3 us
  waiting for transfers between devices: 3.55 us -> 2.86 us
    pallas_call x1, Pallas kernels: 9.91 us -> 11.8 us  [network(): pl.pallas_call(kernel, grid=(count // ROWS_MLP,), out_shape=(jax.ShapeDty...]
    all_to_all x2, waiting for transfers between devices: 2.21 us -> 1.53 us  [exchange(): lax.all_to_all(rows, GROUP_AXES, split_axis=0, concat_axis=0, tiled=True)]
    pallas_call x1, Pallas kernels: 9.16 us -> 9.83 us  [dispatch(): pl.pallas_call(kernel, out_shape=(shape((count, width), jnp.bfloat16), sh...]
  transfers between devices with their start and end apart: 6 -> 6, of which waited for: 2 -> 2; matrix products, arithmetic and copies ran while one was open for 0% -> 0% of each run, Pallas kernels for 49% -> 52%
where the time goes in v7:
time: 61.7 us; the launch traced here: 60.5 us
  Pallas kernels  31.3 us (51%)
  starting transfers between devices  24 us (39%)
  waiting for transfers between devices  2.86 us (5%)
  local copies, waits for them, and re-layouts  1.55 us (3%)
  between operations  0.76 us (1%)
    all_to_all x2, starting transfers between devices, exchange(): lax.all_to_all(rows, GROUP_AXES, split_axis=0, concat_axis=0, tiled=True)  13.3 us
    pallas_call x1, Pallas kernels, network(): pl.pallas_call(kernel, grid=(count // ROWS_MLP,), out_shape=(jax.ShapeDty...  11.8 us
    ppermute x4, starting transfers between devices, swapped(): return lax.ppermute(edge, axis, pairs + [(j, i) for i, j in pairs])  10.7 us
    pallas_call x1, Pallas kernels, dispatch(): pl.pallas_call(kernel, out_shape=(shape((count, width), jnp.bfloat16), sh...  9.83 us
    pallas_call x1, Pallas kernels, finish(): pl.pallas_call(kernel, out_shape=jax.ShapeDtypeStruct(state.shape, jnp.fl...  9.72 us
    unnamed x11, local copies, waits for them, and re-layouts  1.55 us
    all_to_all x2, waiting for transfers between devices, exchange(): lax.all_to_all(rows, GROUP_AXES, split_axis=0, concat_axis=0, tiled=True)  1.53 us
    ppermute x4, waiting for transfers between devices, swapped(): return lax.ppermute(edge, axis, pairs + [(j, i) for i, j in pairs])  1.34 us
  transfers between devices with their start and end apart: 6, of which 2 were waited for; matrix products, arithmetic and copies ran while one was open for 0% of the time, Pallas kernels for 52%

profile of v7, /device:TPU:2, one launch (start us, length us, event | category | flops | bytes accessed | tf_op | source)
XLA Modules:
  0.0 60.5 jit_solution(9318166007222191167)
XLA Ops:
  0.6 7.7 %all-to-all-start = ((bf16[32,128,128]{2,1,0:T(8,128)(2,1)}), bf16[32,128,128]{2,1,0:T(8,128)(2,1)}, u32[]{:S(2)}, u32[]{:S(2)}) async-start(bf16[32,128,128]{2,1,0:T(8,128)(2,1)} %bitcast.20), calls=%async_computation | async-start | bytes 2097152 | tf_op jit(solution)/shard_map/all_to_all | solution.py:23
  8.3 9.8 %dispatch.1 = (bf16[4096,128]{1,0:T(8,128)(2,1)}, bf16[128,256]{1,0:T(8,128)(2,1)}, bf16[128,256]{1,0:T(8,128)(2,1)}, bf16[16,128]{1,0:T(8,128)(2,1)}, bf16[16,1...) custom-call(s32[16,256]{1,0:T(8,128)} %refs_0_.1, ...), custom_call_target="tpu_custom_call" | custom-call | flops 4294967296 | bytes 3145728 | tf_op jit(solution)/shard_map/dispatch/pallas_call | solution.py:167
  18.2 0.2 collective-permute-start.2
  18.4 0.4 collective-permute-start
  18.8 4.2 %collective-permute-start.1 = (bf16[128,256]{1,0:T(8,128)(2,1)}, bf16[128,256]{1,0:T(8,128)(2,1)S(1)}, u32[]{:S(2)}, u32[]{:S(2)}) collective-permute-start(bf16[128,256]{1,0:T(8,128)(2,1)} %get-tuple-element.27), channel_id=1, source_target_pairs={{2,4},{6,8},{10,12},{14,16},{18,20},{22,24},{26,28},{4,2},{8,6},{1... | collective-permute-start | bytes 196616 | tf_op jit(solution)/shard_map/ppermute | solution.py:19
  23.0 1.5 %all-to-all-done = bf16[32,128,128]{2,1,0:T(8,128)(2,1)} async-done(((bf16[32,128,128]{2,1,0:T(8,128)(2,1)}), bf16[32,128,128]{2,1,0:T(8,128)(2,1)}, u32[]{:S(2)}, u32[]{:S(2)}) %all-to-all-start) | async-done | bytes 1048608 | tf_op jit(solution)/shard_map/all_to_all | solution.py:23
  24.5 11.8 %network.1 = (bf16[4096,128]{1,0:T(8,128)(2,1)}, bf16[4096,128]{1,0:T(8,128)(2,1)}) custom-call(s32[32,128]{1,0:T(8,128)} %get-tuple-element.19.refs_0_, bf16[4096,128]{1,0:T(8,128)(2,1)} %get-tuple-element.20.refs_1_, bf16[4096,128]{1,0:T(8,128)(2,1)} %bitcast.4.refs_2_, bf16[256,512]{1,0:T(8,128)(2,1)} %get-tuple-element.21.refs_3_, ...), custom_call_target="tpu_custom_call" | custom-call | flops 6442450944 | bytes 5767168 | tf_op jit(solution)/shard_map/network/pallas_call | solution.py:277
  36.3 0.0 copy-start.3
  36.3 0.0 collective-permute-done.2.refs_6_
  36.3 0.0 copy-start.2
  36.3 0.0 collective-permute-done.refs_4_
  36.3 0.0 copy-start
  36.3 0.0 collective-permute-done.1.refs_5_
  36.3 0.0 copy-start.1
  36.4 5.7 %all-to-all-start.1 = ((bf16[32,128,128]{2,1,0:T(8,128)(2,1)}), bf16[32,128,128]{2,1,0:T(8,128)(2,1)S(1)}, u32[]{:S(2)}, u32[]{:S(2)}) async-start(bf16[32,128,128]{2,1,0:T(8,128)(2,1)} %bitcast.21), calls=%async_computation.1 | async-start | bytes 2097152 | tf_op jit(solution)/shard_map/all_to_all | solution.py:23
  42.0 0.0 copy-done.3
  42.0 5.9 %collective-permute-start.3 = (bf16[16,128]{1,0:T(8,128)(2,1)S(1)}, bf16[16,128]{1,0:T(8,128)(2,1)S(1)}, u32[]{:S(2)}, u32[]{:S(2)}) collective-permute-start(bf16[16,128]{1,0:T(8,128)(2,1)S(1)} %copy-done.3), channel_id=1, source_target_pairs={{1,32},{33,64},{65,96},{97,128},{129,160},{161,192},{193,224},{225... | collective-permute-start | bytes 12296 | tf_op jit(solution)/shard_map/ppermute | solution.py:19
  47.9 1.3 %collective-permute-done.3.refs_7_ = bf16[16,128]{1,0:T(8,128)(2,1)S(1)} collective-permute-done((bf16[16,128]{1,0:T(8,128)(2,1)S(1)}, bf16[16,128]{1,0:T(8,128)(2,1)S(1)}, u32[]{:S(2)}, u32[]{:S(2)}) %collective-permute-start.3) | collective-permute-done | bytes 4128 | tf_op jit(solution)/shard_map/ppermute | solution.py:19
  49.3 0.0 copy-done.2
  49.3 0.0 copy-done.1
  49.3 0.6 copy-done.4
  49.8 9.7 %finish.1 = f32[4096,128]{1,0:T(8,128)} custom-call(s32[2,16,128]{2,1,0:T(8,128)} %get-tuple-element.18.refs_0_, bf16[4096,128]{1,0:T(8,128)(2,1)} %get-tuple-element.24.refs_1_, f32[4096,128]{1,0:T(8,128)} %bitcast.23, f32[4096,128]{1,0:T(8,128)} %bitcast.24, bf16[128,256]{1,0:T(8,128)(2,1)} %copy-done, bf16[128,256]{1,0:T(8,128)(2,1)} %copy-done.1, ...), custom_call_target="tpu_custom_call" | custom-call | flops 4294967296 | bytes 7340032 | tf_op jit(solution)/shard_map/finish/pallas_call | solution.py:435
  59.6 0.0 all-to-all-done.1
  59.6 1.0 %copy.13 = bf16[4096,128]{1,0:T(8,128)(2,1)} copy(bf16[4096,128]{1,0:T(8,128)(2,1)S(1)} %bitcast.19) | data formatting | bytes 2097152
  (2 shorter events, 0.0 us)
Async XLA Ops:
  0.6 23.9 %all-to-all-start = ((bf16[32,128,128]{2,1,0:T(8,128)(2,1)}), bf16[32,128,128]{2,1,0:T(8,128)(2,1)}, u32[]{:S(2)}, u32[]{:S(2)}) async-start(bf16[32,128,128]{2,1,0:T(8,128)(2,1)} %bitcast.20), calls=%async_computation | async-start | bytes 2097152 | tf_op jit(solution)/shard_map/all_to_all | solution.py:23
  18.2 18.1 %collective-permute-start.2 = (bf16[16,128]{1,0:T(8,128)(2,1)}, bf16[16,128]{1,0:T(8,128)(2,1)S(1)}, u32[]{:S(2)}, u32[]{:S(2)}) collective-permute-start(bf16[16,128]{1,0:T(8,128)(2,1)} %get-tuple-element.28), channel_id=1, source_target_pairs={{0,1},{32,33},{64,65},{96,97},{128,129},{160,161},{192,193},{224,2... | collective-permute-start | bytes 12296 | tf_op jit(solution)/shard_map/ppermute | solution.py:19
  18.4 17.9 %collective-permute-start = (bf16[128,256]{1,0:T(8,128)(2,1)}, bf16[128,256]{1,0:T(8,128)(2,1)S(1)}, u32[]{:S(2)}, u32[]{:S(2)}) collective-permute-start(bf16[128,256]{1,0:T(8,128)(2,1)} %get-tuple-element.26), channel_id=1, source_target_pairs={{0,2},{4,6},{8,10},{12,14},{16,18},{20,22},{24,26},{28,30},{2,0},{... | collective-permute-start | bytes 196616 | tf_op jit(solution)/shard_map/ppermute | solution.py:19
  18.8 17.6 %collective-permute-start.1 = (bf16[128,256]{1,0:T(8,128)(2,1)}, bf16[128,256]{1,0:T(8,128)(2,1)S(1)}, u32[]{:S(2)}, u32[]{:S(2)}) collective-permute-start(bf16[128,256]{1,0:T(8,128)(2,1)} %get-tuple-element.27), channel_id=1, source_target_pairs={{2,4},{6,8},{10,12},{14,16},{18,20},{22,24},{26,28},{4,2},{8,6},{1... | collective-permute-start | bytes 196616 | tf_op jit(solution)/shard_map/ppermute | solution.py:19
  36.3 5.7 %copy-start.3 = (bf16[16,128]{1,0:T(8,128)(2,1)S(1)}, bf16[16,128]{1,0:T(8,128)(2,1)}, u32[]{:S(2)}) copy-start(bf16[16,128]{1,0:T(8,128)(2,1)} %get-tuple-element.32) | copy-start | bytes 12292
  36.3 13.0 %copy-start.2 = (bf16[16,128]{1,0:T(8,128)(2,1)}, bf16[16,128]{1,0:T(8,128)(2,1)S(1)}, u32[]{:S(2)}) copy-start(bf16[16,128]{1,0:T(8,128)(2,1)S(1)} %collective-permute-done.2.refs_6_) | copy-start | bytes 12292
  36.3 12.9 %copy-start = (bf16[128,256]{1,0:T(8,128)(2,1)}, bf16[128,256]{1,0:T(8,128)(2,1)S(1)}, u32[]{:S(2)}) copy-start(bf16[128,256]{1,0:T(8,128)(2,1)S(1)} %collective-permute-done.refs_4_) | copy-start | bytes 196612
  36.3 12.9 %copy-start.1 = (bf16[128,256]{1,0:T(8,128)(2,1)}, bf16[128,256]{1,0:T(8,128)(2,1)S(1)}, u32[]{:S(2)}) copy-start(bf16[128,256]{1,0:T(8,128)(2,1)S(1)} %collective-permute-done.1.refs_5_) | copy-start | bytes 196612
  36.4 23.2 %all-to-all-start.1 = ((bf16[32,128,128]{2,1,0:T(8,128)(2,1)}), bf16[32,128,128]{2,1,0:T(8,128)(2,1)S(1)}, u32[]{:S(2)}, u32[]{:S(2)}) async-start(bf16[32,128,128]{2,1,0:T(8,128)(2,1)} %bitcast.21), calls=%async_computation.1 | async-start | bytes 2097152 | tf_op jit(solution)/shard_map/all_to_all | solution.py:23
  42.0 7.2 %collective-permute-start.3 = (bf16[16,128]{1,0:T(8,128)(2,1)S(1)}, bf16[16,128]{1,0:T(8,128)(2,1)S(1)}, u32[]{:S(2)}, u32[]{:S(2)}) collective-permute-start(bf16[16,128]{1,0:T(8,128)(2,1)S(1)} %copy-done.3), channel_id=1, source_target_pairs={{1,32},{33,64},{65,96},{97,128},{129,160},{161,192},{193,224},{225... | collective-permute-start | bytes 12296 | tf_op jit(solution)/shard_map/ppermute | solution.py:19
  49.3 0.6 copy-start.4
